TPU v7x, 128 devices: a whole 4x4x4 slice. The times are simulated.
128 devices in a mesh: box: 16 (over x, y), bal: 8 (over z, core).
Axes of the slice: x: 4, y: 4, z: 4, core: 2. Of those that a mesh axis runs over, the one named last changes fastest.
Arguments:
- species_state: bfloat16 [512, 218, 1024], P('box', None, 'bal'), may hold values from -6 to 6
- stiffness: int32 [512, 8], P('box', 'bal'), may hold values from 6 to 12
- send_list: int32 [16, 8, 16, 4], P('box', 'bal'), may hold values from -1 to 31, as said below
- jacobian: bfloat16 [1024, 8, 256, 256], P('box', 'bal'), may hold values from -0.375 to 0.375
- pattern: int32 [1024, 8, 4, 4], P('box', 'bal'), may hold values 0 or 1
- diffusivity: float32 [218], replicated, may hold values from 0.02 to 0.24
Outputs:
- species_field: float32 [512, 218, 1024], P('box', None, 'bal')
Inputs may be any that keep to these rules, and one draw needn't show every extreme that they name: `send_list`: in the table of device (b, j), entry (o, c) is the local tile that goes to slot c of owner o in the same j, or -1 for an empty slot. Every local tile stands exactly once in its device's table. In every j, one owner has all 4 slots from every device filled. Any slot of the other owners may be filled or empty.
All inputs are finite; a program needn't handle non-finite values. No bound on the sum of `pattern` on one device may be relied on, other than what follows from the above.
Results may differ from a plain program's by a relative error of at most 0.0003.
Values may be sent and summed in bfloat16 or wider, within the bound.
No kernel may reach another device: no remote copies, remote signals or barrier semaphores. Data moves between devices by JAX's collectives and lax.ppermute only.
A program may use at most 128 MiB of HBM per device.

v0:
```python
import jax
import jax.numpy as jnp
from jax import lax
from jax.sharding import PartitionSpec as P

S = 218
BL = 64
DSTEPS = 2
SP = 256


epsilon = 1e-06
batch_rows = 8


def with_halo(block, sides, width):
    for axis, dim in sides:
        count = lax.axis_size(axis)
        forward = [(i, i + 1) for i in range(count - 1)]
        backward = [(target, source) for source, target in forward]
        low = lax.ppermute(
            lax.slice_in_dim(block, block.shape[dim] - width, None, axis=dim), axis, forward
        )
        high = lax.ppermute(lax.slice_in_dim(block, 0, width, axis=dim), axis, backward)
        block = jnp.concatenate([low, block, high], axis=dim)
    return block


def masked_operator(jac_block, blocks):
    expanded = jnp.repeat(jnp.repeat(blocks.astype(jnp.float32), BL, axis=-2), BL, axis=-1)
    inside = (jnp.arange(SP) < S).astype(jnp.float32)
    return jac_block.astype(jnp.float32) * expanded * inside[:, None] * inside[None, :]


def solve_batch(tile_data, operator, counts):
    start_value = jnp.pad(tile_data.astype(jnp.float32), ((0, 0), (0, SP - S), (0, 0)))
    remainder = jnp.einsum("nij,njc->nic", operator, start_value, precision=lax.Precision.HIGHEST)

    def advance(turn_no, state_pair):
        guess, left_over = state_pair
        mapped = left_over - jnp.einsum(
            "nij,njc->nic", operator, left_over, precision=lax.Precision.HIGHEST
        )
        step_size = jnp.sum(left_over * mapped, axis=1, keepdims=True) / (
            jnp.sum(mapped * mapped, axis=1, keepdims=True) + epsilon
        )
        active = (turn_no < counts)[:, None, None]
        return (
            jnp.where(active, guess + step_size * left_over, guess),
            jnp.where(active, left_over - step_size * mapped, left_over),
        )

    guess, left_over = lax.fori_loop(0, jnp.max(counts), advance, (start_value, remainder))
    return guess[:, :S]


def solve_sorted(tile_data, jac_blocks, block_masks, counts):
    total = counts.shape[0]
    order = jnp.argsort(-counts, stable=True)
    batches = order.reshape(total // batch_rows, batch_rows)

    def one_batch(picked):
        return solve_batch(
            jnp.take(tile_data, picked, axis=0),
            masked_operator(
                jnp.take(jac_blocks, picked, axis=0), jnp.take(block_masks, picked, axis=0)
            ),
            jnp.take(counts, picked, axis=0),
        )

    solved = lax.map(one_batch, batches).reshape(total, S, tile_data.shape[2])
    return jnp.zeros_like(solved).at[order].set(solved)


def neighbour_sum(padded):
    return padded[2:, :, 1:-1] + padded[:-2, :, 1:-1] + padded[1:-1, :, 2:] + padded[1:-1, :, :-2]


def on_device(species_state, stiffness, send_list, jacobian, pattern, diffusivity):
    box_count = lax.axis_size("box")
    tiles_dev = species_state.shape[0]
    tile_width = species_state.shape[2]
    slots_dev = jacobian.shape[0]
    slots_cap = slots_dev // box_count
    slot_list = send_list.reshape(slots_dev)
    is_live = slot_list >= 0
    slot_tile = jnp.where(is_live, slot_list, 0)
    target = jnp.where(is_live, slot_list, tiles_dev)
    counts = stiffness[:, 0]
    packed = jnp.take(species_state, slot_tile, axis=0) * is_live[:, None, None].astype(
        species_state.dtype
    )
    packed_counts = jnp.where(is_live, counts[slot_tile], 0)
    arrived, arrived_counts = (
        lax.all_to_all(
            packed.reshape(box_count, slots_cap, S, tile_width),
            "box",
            split_axis=0,
            concat_axis=0,
            tiled=True,
        ),
        lax.all_to_all(
            packed_counts.reshape(box_count, slots_cap),
            "box",
            split_axis=0,
            concat_axis=0,
            tiled=True,
        ),
    )
    solved = solve_sorted(
        arrived.reshape(slots_dev, S, tile_width),
        jacobian[:, 0],
        pattern[:, 0],
        arrived_counts.reshape(slots_dev),
    )
    returned = lax.all_to_all(
        solved.reshape(box_count, slots_cap, S, tile_width),
        "box",
        split_axis=0,
        concat_axis=0,
        tiled=True,
    )
    reacted = (
        jnp.zeros((tiles_dev, S, tile_width), jnp.float32)
        .at[target]
        .set(returned.reshape(slots_dev, S, tile_width), mode="drop")
    )
    diffuse_rate = diffusivity[None, :, None]
    species_field = reacted
    for repeat_no in range(DSTEPS):
        padded = with_halo(species_field, (("box", 0), ("bal", 2)), 1)
        species_field = species_field + diffuse_rate * (neighbour_sum(padded) - 4.0 * species_field)
    return species_field


def solution(mesh):
    in_specs = (
        P("box", None, "bal"),
        P("box", "bal"),
        P("box", "bal", None, None),
        P("box", "bal", None, None),
        P("box", "bal", None, None),
        P(),
    )
    out_specs = P("box", None, "bal")
    return jax.shard_map(
        on_device, mesh=mesh, in_specs=in_specs, out_specs=out_specs, check_vma=False
    )
```

profile of v0, /device:TPU:3, one launch (start us, length us, event | category | flops | bytes accessed | tf_op | source)
XLA Modules:
  0.0 730.3 jit_solution(18328699730081811780)
XLA Ops:
  4.0 6.9 all-to-all-start
  11.6 15.9 %gather_fusion.5 = bf16[64,218,128]{2,0,1:T(8,128)(2,1)} fusion(bf16[32,218,128]{2,0,1:T(8,128)(2,1)S(1)} %copy-done, s32[1024]{0:T(1024)S(1)} %pad_clamp_fusion.1), kind=kCustom, calls=%fused_computation.5 | custom fusion | bytes 7143680 | tf_op jit(solution)/shard_map/jit(_take)/gather | solution.py:90
  27.7 6.3 fusion.16
  34.1 6.8 all-to-all-start.1
  44.4 38.3 %all-to-all-done.1 = bf16[16,4,218,128]{3,1,2,0:T(4,128)(2,1)} async-done(((bf16[16,4,218,128]{3,1,2,0:T(4,128)(2,1)}), bf16[16,4,218,128]{3,1,2,0:T(4,128)(2,1)}, u32[]{:S(2)}, u32[]{:S(2)}) %all-to-all-start.1) | async-done | bytes 3571744 | tf_op jit(solution)/shard_map/all_to_all | solution.py:95
  82.7 4.7 copy.84
  87.4 313.4 %while.34 = (s32[]{:T(128)}, f32[8,8,218,128]{3,2,1,0:T(8,128)}, s32[8,8]{1,0:T(8,128)S(1)}, bf16[64,218,128]{2,1,0:T(8,128)(2,1)}, bf16[64,256,256]{2,1,0:T(8,1...) while((s32[]{:T(128)}, f32[8,8,218,128]{3,2,1,0:T(8,128)}, ...), condition=%wide.region_7.8_spmd, body=%wide.region_1.7_spmd.sunk | while | flops 1616604928 | bytes 31944400 | solution.py:71
  91.7 4.0 gather_fusion.3
  102.7 55.0 %while.35 = (s32[]{:T(128)}, f32[8,256,128]{2,1,0:T(8,128)}, f32[8,256,128]{2,1,0:T(8,128)S(1)}, s32[]{:T(128)}, s32[8]{0:T(128)S(1)}, /*index=5*/f32[8,256,256]{2,1,0:T(8,128)S(1)}, s32[]{:T(128)}) while((s32[]{:T(128)}, f32[8,256,128]{2,1,0:T(8,128)}, f32[8,256,128]{2,1,0:T(8,128)S(1)}, s32[]{:T(128)}, s32[8]{0:T(128)S(1)}, ...), condition=%wide.region_6.6_spmd, body=%wide.region_3.5_spmd.sunk | while | flops 808189952 | bytes 9461889 | solution.py:53
  164.2 4.0 gather_fusion.3
  175.3 44.1 %while.35 = (s32[]{:T(128)}, f32[8,256,128]{2,1,0:T(8,128)}, f32[8,256,128]{2,1,0:T(8,128)S(1)}, s32[]{:T(128)}, s32[8]{0:T(128)S(1)}, /*index=5*/f32[8,256,256]{2,1,0:T(8,128)S(1)}, s32[]{:T(128)}) while((s32[]{:T(128)}, f32[8,256,128]{2,1,0:T(8,128)}, f32[8,256,128]{2,1,0:T(8,128)S(1)}, s32[]{:T(128)}, s32[8]{0:T(128)S(1)}, ...), condition=%wide.region_6.6_spmd, body=%wide.region_3.5_spmd.sunk | while | flops 808189952 | bytes 9461889 | solution.py:53
  225.9 4.0 gather_fusion.3
  236.9 38.7 %while.35 = (s32[]{:T(128)}, f32[8,256,128]{2,1,0:T(8,128)}, f32[8,256,128]{2,1,0:T(8,128)S(1)}, s32[]{:T(128)}, s32[8]{0:T(128)S(1)}, /*index=5*/f32[8,256,256]{2,1,0:T(8,128)S(1)}, s32[]{:T(128)}) while((s32[]{:T(128)}, f32[8,256,128]{2,1,0:T(8,128)}, f32[8,256,128]{2,1,0:T(8,128)S(1)}, s32[]{:T(128)}, s32[8]{0:T(128)S(1)}, ...), condition=%wide.region_6.6_spmd, body=%wide.region_3.5_spmd.sunk | while | flops 808189952 | bytes 9461889 | solution.py:53
  282.1 4.0 gather_fusion.3
  293.1 33.3 %while.35 = (s32[]{:T(128)}, f32[8,256,128]{2,1,0:T(8,128)}, f32[8,256,128]{2,1,0:T(8,128)S(1)}, s32[]{:T(128)}, s32[8]{0:T(128)S(1)}, /*index=5*/f32[8,256,256]{2,1,0:T(8,128)S(1)}, s32[]{:T(128)}) while((s32[]{:T(128)}, f32[8,256,128]{2,1,0:T(8,128)}, f32[8,256,128]{2,1,0:T(8,128)S(1)}, s32[]{:T(128)}, s32[8]{0:T(128)S(1)}, ...), condition=%wide.region_6.6_spmd, body=%wide.region_3.5_spmd.sunk | while | flops 808189952 | bytes 9461889 | solution.py:53
  332.9 4.0 gather_fusion.3
  350.9 4.0 gather_fusion.3
  369.0 4.0 gather_fusion.3
  387.1 4.0 gather_fusion.3
  400.8 3.9 broadcast_in_dim.121
  404.8 15.3 %scatter_fusion = f32[64,218,128]{2,1,0:T(8,128)} fusion(f32[64,218,128]{2,1,0:T(8,128)} %broadcast_in_dim.121, s32[64]{0:T(128)S(1)} %compare_select_fusion.5, f32[64,218,128]{2,1,0:T(8,128)} %bitcast.56), kind=kCustom, calls=%fused_computation.6 | custom fusion | bytes 21430528 | tf_op jit(solution)/shard_map/scatter | solution.py:72
  420.1 7.8 %copy.86 = f32[16,4,218,128]{3,1,2,0:T(4,128)S(1)} copy(f32[16,4,218,128]{3,2,1,0:T(8,128)} %bitcast.52) | data formatting | bytes 14286848 | tf_op jit(solution)/shard_map/reshape | solution.py:117
  427.9 188.6 %all_to_all.16 = f32[16,4,218,128]{3,1,2,0:T(4,128)S(1)} all-to-all(f32[16,4,218,128]{3,1,2,0:T(4,128)S(1)} %copy.86), channel_id=1, replica_groups=mesh['box'=16,'bal'=8] {'box'}, dimensions={0} | all-to-all | bytes 14286848 | tf_op jit(solution)/shard_map/all_to_all | solution.py:116
  616.5 4.0 copy.87
  622.8 14.4 %scatter_fusion.1 = f32[32,218,128]{2,1,0:T(8,128)} fusion(f32[32,218,128]{2,1,0:T(8,128)} %broadcast_in_dim.119, s32[64]{0:T(128)S(1)} %get-tuple-element.181, f32[64,218,128]{2,1,0:T(8,128)} %bitcast.53), kind=kCustom, calls=%fused_computation.7 | custom fusion | bytes 21430528 | tf_op jit(solution)/shard_map/scatter | solution.py:126
  640.1 5.5 collective-permute-start
  648.2 4.6 fusion.21
  669.4 10.4 %fusion.13 = f32[32,218,128]{2,1,0:T(8,128)S(1)} fusion(f32[32,218,128]{2,1,0:T(8,128)} %scatter_fusion.1, f32[34,218,128]{2,1,0:T(8,128)} %copy-done.2, f32[34,218,1]{2,1,0:T(8,128)} %copy.91, f32[34,218,1]{2,1,0:T(8,128)} %copy.89, f32[1,218,128]{2,1,0:T(8,128)S(1)} %collective-permute-done.1, f32[1,218,128]{2,1,0:T(8,128)S(1)} %collective-permute-done, ...), kind=kLoop, calls=%fused_computation.50 | loop fusion | flops 9822208 | bytes 11221768 | tf_op jit(solution)/shard_map/add | solution.py:132
  679.9 5.1 collective-permute-start.4
  687.1 6.2 collective-permute-done.5
  693.6 4.4 fusion.20
  714.4 11.7 %fusion.7 = f32[32,218,128]{2,1,0:T(8,128)S(1)} fusion(f32[32,218,128]{2,1,0:T(8,128)} %copy-done.3, f32[34,218,1]{2,1,0:T(8,128)} %copy.95, f32[1,218,128]{2,1,0:T(8,128)S(1)} %collective-permute-done.4, f32[1,218,128]{2,1,0:T(8,128)S(1)} %collective-permute-done.5, f32[34,218,1]{2,1,0:T(8,128)} %copy.93, f32[218]{0:T(256)S(1)} %copy-done.5), kind=kLoop, calls=%fused_computation.36 | loop fusion | flops 13393920 | bytes 7426824 | tf_op jit(solution)/shard_map/add | solution.py:132
  (344 shorter events, 315.7 us)
Async XLA Ops:
  0.0 11.6 %copy-start = (bf16[32,218,128]{2,0,1:T(8,128)(2,1)S(1)}, bf16[32,218,128]{2,0,1:T(8,128)(2,1)}, u32[]{:S(2)}) copy-start(bf16[32,218,128]{2,0,1:T(8,128)(2,1)} %param.10) | copy-start | bytes 5357572
  4.0 30.1 %all-to-all-start = ((s32[16,1,4]{2,1,0:T(1,128)}), s32[16,1,4]{2,1,0:T(1,128)S(1)}, u32[]{:S(2)}, u32[]{:S(2)}) async-start(s32[16,1,4]{2,1,0:T(1,128)} %copy.80), calls=%async_computation | async-start | bytes 16384 | tf_op jit(solution)/shard_map/all_to_all | solution.py:102
  34.0 6.8 copy-start.4
  34.1 48.7 %all-to-all-start.1 = ((bf16[16,4,218,128]{3,1,2,0:T(4,128)(2,1)}), bf16[16,4,218,128]{3,1,2,0:T(4,128)(2,1)}, u32[]{:S(2)}, u32[]{:S(2)}) async-start(bf16[16,4,218,128]{3,1,2,0:T(4,128)(2,1)} %fusion.16), calls=%async_computation.1 | async-start | bytes 7143424 | tf_op jit(solution)/shard_map/all_to_all | solution.py:95
  638.2 7.6 %collective-permute-start.1 = (f32[1,218,128]{2,1,0:T(8,128)S(1)}, f32[1,218,128]{2,1,0:T(8,128)S(1)}, u32[]{:S(2)}, u32[]{:S(2)}) collective-permute-start(f32[1,218,128]{2,1,0:T(8,128)S(1)} %get-tuple-element.177), channel_id=1, source_target_pairs={{0,8},{8,16},{16,24},{24,32},{32,40},{40,48},{48,56},{56,64},{64,7... | collective-permute-start | bytes 334856 | tf_op jit(solution)/shard_map/ppermute | solution.py:21
  640.1 8.0 %collective-permute-start = (f32[1,218,128]{2,1,0:T(8,128)S(1)}, f32[1,218,128]{2,1,0:T(8,128)S(1)}, u32[]{:S(2)}, u32[]{:S(2)}) collective-permute-start(f32[1,218,128]{2,1,0:T(8,128)S(1)} %get-tuple-element.176), channel_id=1, source_target_pairs={{8,0},{16,8},{24,16},{32,24},{40,32},{48,40},{56,48},{64,56},{72,6... | collective-permute-start | bytes 334856 | tf_op jit(solution)/shard_map/ppermute | solution.py:24
  648.1 4.6 copy-start.2
  655.6 8.6 %collective-permute-start.2 = (f32[34,218,1]{1,2,0:T(1,128)S(1)}, f32[34,218,1]{1,2,0:T(1,128)S(1)}, u32[]{:S(2)}, u32[]{:S(2)}) collective-permute-start(f32[34,218,1]{1,2,0:T(1,128)S(1)} %copy.88), channel_id=1, source_target_pairs={{1,0},{2,1},{3,2},{4,3},{5,4},{6,5},{7,6},{9,8},{10,9},{11,10},{12... | collective-permute-start | bytes 88952 | tf_op jit(solution)/shard_map/ppermute | solution.py:24
  660.4 9.0 %copy-start.5 = (f32[218]{0:T(256)S(1)}, f32[218]{0:T(256)}, u32[]{:S(2)}) copy-start(f32[218]{0:T(256)} %param.15) | copy-start | bytes 2620
  660.4 6.4 collective-permute-start.3
  679.8 13.8 %copy-start.3 = (f32[32,218,128]{2,1,0:T(8,128)}, f32[32,218,128]{2,1,0:T(8,128)S(1)}, u32[]{:S(2)}) copy-start(f32[32,218,128]{2,1,0:T(8,128)S(1)} %fusion.13) | copy-start | bytes 10715140
  679.9 7.3 collective-permute-start.4
  684.9 8.4 %collective-permute-start.5 = (f32[1,218,128]{2,1,0:T(8,128)S(1)}, f32[1,218,128]{2,1,0:T(8,128)S(1)}, u32[]{:S(2)}, u32[]{:S(2)}) collective-permute-start(f32[1,218,128]{2,1,0:T(8,128)S(1)} %get-tuple-element.174), channel_id=1, source_target_pairs={{0,8},{8,16},{16,24},{24,32},{32,40},{40,48},{48,56},{56,64},{64,7... | collective-permute-start | bytes 334856 | tf_op jit(solution)/shard_map/ppermute | solution.py:21
  700.9 8.4 %collective-permute-start.6 = (f32[34,218,1]{1,2,0:T(1,128)S(1)}, f32[34,218,1]{1,2,0:T(1,128)S(1)}, u32[]{:S(2)}, u32[]{:S(2)}) collective-permute-start(f32[34,218,1]{1,2,0:T(1,128)S(1)} %copy.92), channel_id=1, source_target_pairs={{1,0},{2,1},{3,2},{4,3},{5,4},{6,5},{7,6},{9,8},{10,9},{11,10},{12... | collective-permute-start | bytes 88952 | tf_op jit(solution)/shard_map/ppermute | solution.py:24
  705.9 6.0 collective-permute-start.7
  714.4 15.6 %copy-start.1 = (bf16[32,218,128]{2,0,1:T(8,128)(2,1)S(1)}, bf16[32,218,128]{2,0,1:T(8,128)(2,1)}, u32[]{:S(2)}) copy-start(bf16[32,218,128]{2,0,1:T(8,128)(2,1)} %param.10) | copy-start | bytes 5357572
where the time goes:
time: 744 us; the launch traced here: 730 us
  local copies, waits for them, and re-layouts  210 us (28%)
  blocking collectives  189 us (25%)
  other arithmetic  151 us (20%)
  matrix products  72.3 us (10%)
  waiting for transfers between devices  44.8 us (6%)
  starting transfers between devices  39.6 us (5%)
  loops' own time  23.5 us (3%)
    all_to_all x1, blocking collectives, on_device(): lax.all_to_all(solved.reshape(box_count, slots_cap, S, tile_width), 'box'...  189 us
    select_n x31, other arithmetic, advance(): jnp.where(active, left_over - step_size * mapped, left_over)  86.8 us
    dot_general x31, matrix products, advance(): jnp.einsum('nij,njc->nic', operator, left_over, precision=lax.Precision.H...  63.3 us
    all_to_all x1, waiting for transfers between devices, on_device(): lax.all_to_all(packed.reshape(box_count, slots_cap, S, tile_width), 'box'...  38.3 us
    gather x8, local copies, waits for them, and re-layouts, one_batch(): jnp.take(jac_blocks, picked, axis=0)  31.9 us
    another operation x8, loops' own time, solve_batch(): lax.fori_loop(0, jnp.max(counts), advance, (start_value, remainder))  22.9 us
    add x2, other arithmetic, on_device(): species_field + diffuse_rate * (neighbour_sum(padded) - 4.0 * species_field)  22.2 us
    gather x8, local copies, waits for them, and re-layouts, one_batch(): jnp.take(tile_data, picked, axis=0)  21.4 us
  transfers between devices with their start and end apart: 10, of which 3 were waited for; matrix products, arithmetic and copies ran while one was open for 5% of the time, Pallas kernels for 0%

commit v1 on v0

v1 whole, which is shorter than its diff:
```python
import functools

import jax
import jax.numpy as jnp
from jax import lax
from jax.experimental import pallas as pl
from jax.experimental.pallas import tpu as pltpu
from jax.sharding import PartitionSpec as P

S = 218
SR = 224
SP = 256
BL = 64
NB = 4
PACK = 400
LANES = 128
EPSILON = 1e-06
GROUP = 4
CHUNKS = ((0, 2), (2, 2))
VMEM_LIMIT = 56 * 1024 * 1024


def lane_iota(rows):
    return lax.broadcasted_iota(jnp.int32, (rows, LANES), 1)


def pack_kernel(slots, first, pattern_ref, jac_ref, out_ref):
    box = pl.program_id(0)
    low_half = lane_iota(1) < BL
    for slot in range(slots):
        base = (box * 4 + first + slot) * (NB * NB)

        def row_mask(p, half):
            low = pattern_ref[base + p * NB + 2 * half].astype(jnp.float32)
            high = pattern_ref[base + p * NB + 2 * half + 1].astype(jnp.float32)
            return jnp.where(low_half, low, high)

        right = []
        for p in range(NB):
            rows = min(SR, (p + 1) * BL) - p * BL
            span = pl.ds(p * BL, rows)
            left = jac_ref[0, slot, span, 0:LANES].astype(jnp.float32) * row_mask(p, 0)
            part = jac_ref[0, slot, span, LANES:SP].astype(jnp.float32) * row_mask(p, 1)
            if p == NB - 1:
                inside = lax.broadcasted_iota(jnp.int32, (rows, LANES), 0) < S - p * BL
                left = jnp.where(inside, left, 0.0)
                part = jnp.where(inside, part, 0.0)
            out_ref[0, slot, span, :] = left.astype(jnp.bfloat16)
            right.append(part)
        right = jnp.concatenate(right, axis=0)
        half_rows = SR // 2
        lanes = lane_iota(half_rows)
        middle = jnp.where(
            lanes < BL, right[:half_rows], pltpu.roll(right[half_rows:], BL, 1)
        )
        out_ref[0, slot, pl.ds(SR, half_rows), :] = middle.astype(jnp.bfloat16)
        lanes = lane_iota(BL)
        last = jnp.concatenate([right[192:SR], jnp.zeros((32, LANES), jnp.float32)], axis=0)
        edge = jnp.where(
            lanes < 32,
            pltpu.roll(right[0:64], 64, 1),
            jnp.where(
                lanes < 64,
                pltpu.roll(right[64:128], 96, 1),
                jnp.where(lanes < 96, right[128:192], pltpu.roll(last, 32, 1)),
            ),
        )
        out_ref[0, slot, pl.ds(SR + half_rows, BL), :] = edge.astype(jnp.bfloat16)


def pack_chunk(jacobian, pattern_flat, first, slots):
    boxes = jacobian.shape[0]
    return pl.pallas_call(
        functools.partial(pack_kernel, slots, first),
        grid=(boxes,),
        in_specs=[
            pl.BlockSpec(memory_space=pltpu.SMEM),
            pl.BlockSpec((1, slots, SP, SP), lambda b: (b, first // slots, 0, 0)),
        ],
        out_specs=pl.BlockSpec((1, slots, PACK, LANES), lambda b: (b, 0, 0, 0)),
        out_shape=jax.ShapeDtypeStruct((boxes, slots, PACK, LANES), jnp.bfloat16),
        compiler_params=pltpu.CompilerParams(vmem_limit_bytes=VMEM_LIMIT),
        cost_estimate=pl.CostEstimate(
            flops=0, bytes_accessed=boxes * slots * 230000, transcendentals=0
        ),
        name="pack_chunk",
    )(pattern_flat, jacobian)


def unpack(packed_ref, item, dense_ref, member):
    half_rows = SR // 2
    dense_ref[member, :, 0:LANES] = packed_ref[item, pl.ds(0, SR), :]
    middle = packed_ref[item, pl.ds(SR, half_rows), :].astype(jnp.float32)
    edge = packed_ref[item, pl.ds(SR + half_rows, BL), :].astype(jnp.float32)
    high = pltpu.roll(middle, BL, 1)

    def put(row, rows, low, rest):
        lanes = lane_iota(rows)
        dense_ref[member, pl.ds(row, rows), LANES:SP] = jnp.where(
            lanes < BL, low, rest
        ).astype(jnp.bfloat16)

    put(0, 64, middle[0:64], pltpu.roll(edge, 64, 1))
    shifted = pltpu.roll(edge, 32, 1)
    put(64, 48, middle[64:112], shifted[0:48])
    put(112, 16, high[0:16], shifted[48:64])
    put(128, 64, high[16:80], edge)
    put(192, 32, high[80:112], pltpu.roll(edge[0:32], 96, 1))


def solve_kernel(items, first_call, *refs):
    if first_call:
        plan_ref, packed_hbm, state_hbm, out_hbm, edge_ref = refs[:5]
        scratch = refs[5:]
    else:
        plan_ref, packed_hbm, state_hbm, _, edge_in, out_hbm, edge_ref = refs[:7]
        scratch = refs[7:]
    packed, state, dense, right, left_over, mapped_ref, guess, arrived, state_sem, sent = scratch
    live = plan_ref[3 * items]
    groups = (live + GROUP - 1) // GROUP

    def fetch(place):
        source = plan_ref[place]
        return pltpu.make_async_copy(
            packed_hbm.at[source], packed.at[place], arrived.at[place]
        )

    def start_fetch(place, carry):
        fetch(place).start()
        return carry

    lax.fori_loop(0, groups * GROUP, start_fetch, 0)
    state_copy = pltpu.make_async_copy(state_hbm, state, state_sem)
    state_copy.start()
    right[...] = jnp.zeros_like(right)
    if first_call:
        edge_ref[...] = jnp.zeros_like(edge_ref)
    else:
        edge_ref[...] = edge_in[...]
    state_copy.wait()
    edge_lane = lane_iota(SR) // 4

    def send(buffer, member, tile):
        return pltpu.make_async_copy(
            guess.at[buffer, member], out_hbm.at[tile], sent.at[buffer, member]
        )

    def drain(group_no):
        for member in range(GROUP):
            place = group_no * GROUP + member

            @pl.when(place < live)
            def _():
                send(group_no % 2, member, plan_ref[items + place]).wait()

    def one_group(group_no, carry):
        buffer = group_no % 2
        places = [group_no * GROUP + member for member in range(GROUP)]
        tiles = [plan_ref[items + place] for place in places]
        counts = [plan_ref[2 * items + place] for place in places]

        @pl.when(group_no >= 2)
        def _():
            drain(group_no - 2)

        for member in range(GROUP):
            fetch(places[member]).wait()
        for member in range(GROUP):
            unpack(packed, places[member], dense, member)
        for member in range(GROUP):
            source = jnp.minimum(tiles[member], state.shape[0] - 1)
            start_value = state[source]
            right[member, 0:SR, 0:LANES] = start_value
            guess[buffer, member] = start_value.astype(jnp.float32)
        for member in range(GROUP):
            remainder = jnp.dot(
                dense[member], right[member, :, 0:LANES], preferred_element_type=jnp.float32
            )
            left_over[member] = remainder
            high = remainder.astype(jnp.bfloat16)
            right[member, 0:SR, 0:LANES] = high
            right[member, 0:SR, LANES:SP] = (remainder - high.astype(jnp.float32)).astype(
                jnp.bfloat16
            )

        def advance(turn_no, inner):
            for member in range(GROUP):
                product = jnp.dot(
                    dense[member], right[member], preferred_element_type=jnp.float32
                )
                remainder = left_over[member]
                mapped = remainder - (product[:, 0:LANES] + product[:, LANES:SP])
                mapped_ref[member] = mapped
                above = jnp.sum(remainder * mapped, axis=0, keepdims=True)
                below = jnp.sum(mapped * mapped, axis=0, keepdims=True) + EPSILON
                step = jnp.where(turn_no < counts[member], above / below, 0.0)
                guess[buffer, member] += step * remainder
                remainder = remainder - step * mapped_ref[member]
                left_over[member] = remainder
                high = remainder.astype(jnp.bfloat16)
                right[member, 0:SR, 0:LANES] = high
                right[member, 0:SR, LANES:SP] = (
                    remainder - high.astype(jnp.float32)
                ).astype(jnp.bfloat16)
            return inner

        lax.fori_loop(0, counts[0], advance, 0)
        for member in range(GROUP):
            result = guess[buffer, member]
            tile = tiles[member]
            edge_ref[...] = jnp.where(
                edge_lane == tile, pltpu.roll(result, (4 * tile + 2) % LANES, 1), edge_ref[...]
            )

            @pl.when(places[member] < live)
            def _():
                send(buffer, member, tile).start()
        return carry

    lax.fori_loop(0, groups, one_group, 0)

    for back in range(2):
        @pl.when(groups > back)
        def _():
            drain(groups - 1 - back)


def solve_chunk(plan, packed, state, reacted, edge):
    items = packed.shape[0]
    tiles = state.shape[0]
    first_call = reacted is None
    out_shape = (
        jax.ShapeDtypeStruct((tiles, SR, LANES), jnp.float32),
        jax.ShapeDtypeStruct((SR, LANES), jnp.float32),
    )
    hbm = pl.BlockSpec(memory_space=pl.ANY)
    vmem = pl.BlockSpec(memory_space=pltpu.VMEM)
    in_specs = [pl.BlockSpec(memory_space=pltpu.SMEM), hbm, hbm]
    operands = [plan, packed, state]
    aliases = {}
    if not first_call:
        in_specs += [hbm, vmem]
        operands += [reacted, edge]
        aliases = {3: 0}
    return pl.pallas_call(
        functools.partial(solve_kernel, items, first_call),
        in_specs=in_specs,
        out_specs=(hbm, vmem),
        out_shape=out_shape,
        input_output_aliases=aliases,
        scratch_shapes=[
            pltpu.VMEM((items, PACK, LANES), jnp.bfloat16),
            pltpu.VMEM((tiles, SR, LANES), jnp.bfloat16),
            pltpu.VMEM((GROUP, SR, SP), jnp.bfloat16),
            pltpu.VMEM((GROUP, SP, SP), jnp.bfloat16),
            pltpu.VMEM((GROUP, SR, LANES), jnp.float32),
            pltpu.VMEM((GROUP, SR, LANES), jnp.float32),
            pltpu.VMEM((2, GROUP, SR, LANES), jnp.float32),
            pltpu.SemaphoreType.DMA((items,)),
            pltpu.SemaphoreType.DMA,
            pltpu.SemaphoreType.DMA((2, GROUP)),
        ],
        compiler_params=pltpu.CompilerParams(vmem_limit_bytes=VMEM_LIMIT),
        cost_estimate=pl.CostEstimate(
            flops=items * 300_000_000, bytes_accessed=items * 200000, transcendentals=0
        ),
        name="solve_chunk",
    )(*operands)


def message_kernel(tiles, block_hbm, low_ref, high_ref, down_ref, up_ref, copied):
    copies = [
        pltpu.make_async_copy(block_hbm.at[tiles - 2 : tiles], down_ref.at[0:2], copied.at[0]),
        pltpu.make_async_copy(block_hbm.at[0:2], up_ref.at[0:2], copied.at[1]),
    ]
    for copy in copies:
        copy.start()
    lanes = lane_iota(SR)
    for row, out_ref in ((tiles - 1, down_ref), (0, up_ref)):
        out_ref[2] = jnp.where(
            lanes == 0,
            pltpu.roll(low_ref[...], (-(4 * row + 1)) % LANES, 1),
            pltpu.roll(high_ref[...], (-(4 * row + 3)) % LANES, 1),
        )
    for copy in copies:
        copy.wait()


def make_messages(block, low, high):
    tiles = block.shape[0]
    vmem = pl.BlockSpec(memory_space=pltpu.VMEM)
    shape = jax.ShapeDtypeStruct((3, SR, LANES), jnp.float32)
    return pl.pallas_call(
        functools.partial(message_kernel, tiles),
        in_specs=[pl.BlockSpec(memory_space=pl.ANY), vmem, vmem],
        out_specs=(vmem, vmem),
        out_shape=(shape, shape),
        scratch_shapes=[pltpu.SemaphoreType.DMA((2,))],
        name="make_messages",
    )(block, low, high)


def diffuse_kernel(tiles, inside_ref, block_hbm, above_ref, below_ref, low_ref, high_ref,
                   own_ref, rate_ref, out_ref, rows, copied):
    copy = pltpu.make_async_copy(block_hbm, rows.at[2 : tiles + 2], copied)
    copy.start()
    rows[0:2] = above_ref[0:2]
    rows[tiles + 2 : tiles + 4] = below_ref[0:2]
    lanes = lane_iota(8)
    column = lanes % 4
    has_above, has_below = inside_ref[0], inside_ref[1]
    has_side = jnp.where(column < 2, inside_ref[2], inside_ref[3])
    copy.wait()

    def slab(start, kept):
        span = pl.ds(start, 8)
        rate = rate_ref[span, :]
        own = own_ref[span, :]
        ghost = jnp.where(column < 2, low_ref[span, :], high_ref[span, :])
        corner_above = above_ref[2, span, :]
        corner_below = below_ref[2, span, :]

        up = pltpu.roll(ghost, 4, 1)
        up = jnp.where(lanes == 1, pltpu.roll(corner_above, 1, 1), up)
        up = jnp.where(lanes == 2, pltpu.roll(corner_above, 3, 1), up)
        down = pltpu.roll(ghost, LANES - 4, 1)
        down = jnp.where(lanes == LANES - 3, pltpu.roll(corner_below, LANES - 3, 1), down)
        down = jnp.where(lanes == LANES - 2, pltpu.roll(corner_below, LANES - 1, 1), down)
        side = jnp.where(
            column == 1,
            pltpu.roll(own, LANES - 1, 1) + pltpu.roll(ghost, 1, 1),
            pltpu.roll(own, 1, 1) + pltpu.roll(ghost, LANES - 1, 1),
        )
        later = (ghost + rate * (up + down + side - 4.0 * ghost)) * has_side

        def swapped(edge):
            return jnp.where(column == 2, pltpu.roll(edge, 1, 1), pltpu.roll(edge, LANES - 1, 1))

        edge_now, edge_later = swapped(ghost), swapped(later)

        def step(middle, over, under, edge):
            left = jnp.where(lanes == 0, edge, pltpu.roll(middle, 1, 1))
            right = jnp.where(lanes == LANES - 1, edge, pltpu.roll(middle, LANES - 1, 1))
            return middle + rate * (over + under + left + right - 4.0 * middle)

        def edge_of(edge, row):
            return pltpu.roll(edge, (-(4 * row + 2)) % LANES, 1)

        def first(row):
            if row == -1:
                edge = corner_above
            elif row == tiles:
                edge = corner_below
            else:
                edge = edge_of(edge_now, row)
            value = step(
                rows[row + 2, span, :], rows[row + 1, span, :], rows[row + 3, span, :], edge
            )
            if row == -1:
                return value * has_above
            if row == tiles:
                return value * has_below
            return value

        over, middle = first(-1), first(0)
        for row in range(tiles):
            under = first(row + 1)
            value = step(middle, over, under, edge_of(edge_later, row))
            out_ref[pl.ds(start * tiles + row, kept, stride=tiles), :] = value[0:kept]
            over, middle = middle, under

    def whole_slab(number, carry):
        slab(pl.multiple_of(number * 8, 8), 8)
        return carry

    lax.fori_loop(0, S // 8, whole_slab, 0)
    if S % 8:
        slab(S // 8 * 8, S % 8)


def diffuse(inside, block, above, below, low, high, own, rate):
    tiles = block.shape[0]
    vmem = pl.BlockSpec(memory_space=pltpu.VMEM)
    return pl.pallas_call(
        functools.partial(diffuse_kernel, tiles),
        in_specs=[
            pl.BlockSpec(memory_space=pltpu.SMEM),
            pl.BlockSpec(memory_space=pl.ANY),
        ]
        + [vmem] * 6,
        out_specs=vmem,
        out_shape=jax.ShapeDtypeStruct((S * tiles, LANES), jnp.float32),
        scratch_shapes=[
            pltpu.VMEM((tiles + 4, SR, LANES), jnp.float32),
            pltpu.SemaphoreType.DMA,
        ],
        compiler_params=pltpu.CompilerParams(vmem_limit_bytes=VMEM_LIMIT),
        name="diffuse",
    )(inside, block, above, below, low, high, own, rate)


def make_plan(slot_tile, counts):
    items = slot_tile.shape[0]
    tiles = counts.shape[0]
    live = slot_tile >= 0
    turns = jnp.where(live, counts[jnp.where(live, slot_tile, 0)], 0)
    _, source, tile, turns = lax.sort(
        (
            jnp.where(live, -turns, 1),
            jnp.arange(items, dtype=jnp.int32),
            jnp.where(live, slot_tile, tiles),
            turns,
        ),
        num_keys=1,
    )
    return jnp.concatenate([source, tile, turns, jnp.sum(live, dtype=jnp.int32)[None]])


def shifted(value, axis, by):
    count = lax.axis_size(axis)
    pairs = [(i, i + by) for i in range(count) if 0 <= i + by < count]
    return lax.ppermute(value, axis, pairs)


def on_device(species_state, stiffness, send_list, jacobian, pattern, diffusivity):
    boxes = lax.axis_size("box")
    tiles = species_state.shape[0]
    slots = jacobian.shape[0] // boxes
    by_box = jacobian.reshape(boxes, slots, SP, SP)
    pattern_flat = pattern.reshape(-1)
    received = []
    for first, count in CHUNKS:
        packed = pack_chunk(by_box, pattern_flat, first, count)
        arrived = lax.all_to_all(packed, "box", split_axis=0, concat_axis=0, tiled=True)
        received.append(arrived.reshape(boxes * count, PACK, LANES))

    counts = stiffness[:, 0]
    table = send_list.reshape(boxes, slots)
    plans = [
        make_plan(table[:, first : first + count].reshape(-1), counts) for first, count in CHUNKS
    ]
    state = jnp.pad(species_state, ((0, 0), (0, SR - S), (0, 0)))
    reacted = edge = None
    for plan, packed in zip(plans, received):
        reacted, edge = solve_chunk(plan, packed, state, reacted, edge)

    low = shifted(edge, "bal", 1)
    high = shifted(edge, "bal", -1)
    down, up = make_messages(reacted, low, high)
    above = shifted(down, "box", 1)
    below = shifted(up, "box", -1)
    place = lax.axis_index("box"), lax.axis_index("bal")
    inside = jnp.stack(
        [
            place[0] > 0,
            place[0] < boxes - 1,
            place[1] > 0,
            place[1] < lax.axis_size("bal") - 1,
        ]
    ).astype(jnp.float32)
    rate = jnp.broadcast_to(jnp.pad(diffusivity, (0, SR - S))[:, None], (SR, LANES))
    field = diffuse(inside, reacted, above, below, low, high, edge, rate)
    return field.reshape(S, tiles, LANES).transpose(1, 0, 2)


def solution(mesh):
    in_specs = (
        P("box", None, "bal"),
        P("box", "bal"),
        P("box", "bal", None, None),
        P("box", "bal", None, None),
        P("box", "bal", None, None),
        P(),
    )
    return jax.shard_map(
        on_device,
        mesh=mesh,
        in_specs=in_specs,
        out_specs=P("box", None, "bal"),
        check_vma=False,
    )
```

time: 744 us -> 191 us (0.26)
  the two profiles are of different devices: /device:TPU:3 before, /device:TPU:59 now
where the time goes in v1:
time: 191 us
  Pallas kernels  81.6 us (43%)
  waiting for transfers between devices  57.6 us (30%)
  starting transfers between devices  36.3 us (19%)
  local copies, waits for them, and re-layouts  8.5 us (4%)
  other arithmetic  7.13 us (4%)
    all_to_all x2, waiting for transfers between devices, on_device(): lax.all_to_all(packed, 'box', split_axis=0, concat_axis=0, tiled=True)  42.5 us
    pallas_call x2, Pallas kernels, solve_chunk(): pl.pallas_call(functools.partial(solve_kernel, items, first_call), in_spe...  39.7 us
    ppermute x4, starting transfers between devices, shifted(): return lax.ppermute(value, axis, pairs)  21.5 us
    pallas_call x2, Pallas kernels, pack_chunk(): pl.pallas_call(functools.partial(pack_kernel, slots, first), grid=(boxes,...  21.5 us
    pallas_call x1, Pallas kernels, diffuse(): pl.pallas_call(functools.partial(diffuse_kernel, tiles), in_specs=[pl.Blo...  17.5 us
    ppermute x4, waiting for transfers between devices, shifted(): return lax.ppermute(value, axis, pairs)  15.1 us
    all_to_all x2, starting transfers between devices, on_device(): lax.all_to_all(packed, 'box', split_axis=0, concat_axis=0, tiled=True)  14.8 us
  transfers between devices with their start and end apart: 6, of which 6 were waited for; matrix products, arithmetic and copies ran while one was open for 7% of the time, Pallas kernels for 15%

profile of v1, /device:TPU:59, one launch (start us, length us, event | category | flops | bytes accessed | tf_op | source)
XLA Modules:
  0.0 191.2 jit_solution(12920880076951748989)
XLA Ops:
  0.0 0.8 copy.15
  0.8 0.7 reshape.88.pattern_ref
  1.6 10.7 %pack_chunk.3 = bf16[16,2,400,128]{3,2,1,0:T(8,128)(2,1)} custom-call(s32[1024]{0:T(1024)} %reshape.88.pattern_ref, bf16[16,4,256,256]{3,2,1,0:T(8,128)(2,1)} %bitcast.22), custom_call_target="tpu_custom_call" | custom-call | bytes 7360000 | tf_op jit(solution)/shard_map/pack_chunk/pallas_call | solution.py:73
  12.3 6.6 %all-to-all-start.1 = ((bf16[16,2,400,128]{3,2,1,0:T(8,128)(2,1)}), bf16[16,2,400,128]{3,2,1,0:T(8,128)(2,1)S(1)}, u32[]{:S(2)}, u32[]{:S(2)}) async-start(bf16[16,2,400,128]{3,2,1,0:T(8,128)(2,1)} %pack_chunk.3), calls=%async_computation.1 | async-start | bytes 6553600 | tf_op jit(solution)/shard_map/all_to_all | solution.py:434
  18.9 10.7 %pack_chunk.2 = bf16[16,2,400,128]{3,2,1,0:T(8,128)(2,1)} custom-call(s32[1024]{0:T(1024)} %reshape.88.pattern_ref, bf16[16,4,256,256]{3,2,1,0:T(8,128)(2,1)} %bitcast.23), custom_call_target="tpu_custom_call" | custom-call | bytes 7360000 | tf_op jit(solution)/shard_map/pack_chunk/pallas_call | solution.py:73
  29.7 32.6 %all-to-all-done.1 = bf16[16,2,400,128]{3,2,1,0:T(8,128)(2,1)S(1)} async-done(((bf16[16,2,400,128]{3,2,1,0:T(8,128)(2,1)}), bf16[16,2,400,128]{3,2,1,0:T(8,128)(2,1)S(1)}, u32[]{:S(2)}, u32[]{:S(2)}) %all-to-all-start.1) | async-done | bytes 3276832 | tf_op jit(solution)/shard_map/all_to_all | solution.py:434
  62.2 8.2 %all-to-all-start = ((bf16[16,2,400,128]{3,2,1,0:T(8,128)(2,1)}), bf16[16,2,400,128]{3,2,1,0:T(8,128)(2,1)}, u32[]{:S(2)}, u32[]{:S(2)}) async-start(bf16[16,2,400,128]{3,2,1,0:T(8,128)(2,1)} %pack_chunk.2), calls=%async_computation | async-start | bytes 6553600 | tf_op jit(solution)/shard_map/all_to_all | solution.py:434
  70.5 0.7 fusion.1
  71.7 2.2 %copy.16 = bf16[32,218,128]{2,1,0:T(8,128)(2,1)S(1)} copy(bf16[32,218,128]{2,0,1:T(8,128)(2,1)} %param.6) | data formatting | bytes 3571712 | tf_op args[0]
  73.9 0.7 gather_fusion.1
  74.7 0.7 gather_fusion
  75.4 1.4 pad.8.refs_2_
  76.7 1.6 sort.55
  78.3 1.6 sort.54
  79.9 1.3 pad_add_fusion.1.refs_0_
  81.2 1.3 pad_add_fusion.refs_0_
  82.6 18.0 %solve_chunk.2 = (f32[32,224,128]{2,1,0:T(8,128)}, f32[224,128]{1,0:T(8,128)}) custom-call(s32[97]{0:T(128)} %pad_add_fusion.1.refs_0_, bf16[32,400,128]{2,1,0:T(8,128)(2,1)} %bitcast.24, bf16[32,224,128]{2,1,0:T(8,128)(2,1)} %pad.8.refs_2_), custom_call_target="tpu_custom_call" | custom-call | flops 9600000000 | bytes 6400000 | tf_op jit(solution)/shard_map/solve_chunk/pallas_call | solution.py:245
  100.5 9.9 %all-to-all-done = bf16[16,2,400,128]{3,2,1,0:T(8,128)(2,1)} async-done(((bf16[16,2,400,128]{3,2,1,0:T(8,128)(2,1)}), bf16[16,2,400,128]{3,2,1,0:T(8,128)(2,1)}, u32[]{:S(2)}, u32[]{:S(2)}) %all-to-all-start) | async-done | bytes 3276832 | tf_op jit(solution)/shard_map/all_to_all | solution.py:434
  110.4 21.7 %solve_chunk.3 = (f32[32,224,128]{2,1,0:T(8,128)}, f32[224,128]{1,0:T(8,128)}) custom-call(s32[97]{0:T(128)} %pad_add_fusion.refs_0_, bf16[32,400,128]{2,1,0:T(8,128)(2,1)} %bitcast.9.refs_1_, bf16[32,224,128]{2,1,0:T(8,128)(2,1)} %pad.8.refs_2_, f32[32,224,128]{2,1,0:T(8,128)} %get-tuple-element.23.refs_3_, ...), custom_call_target="tpu_custom_call", output_to_operand_aliasing={{0}: (3, {})} | custom-call | flops 9600000000 | bytes 6400000 | tf_op jit(solution)/shard_map/solve_chunk/pallas_call | solution.py:245
  132.2 11.0 %collective-permute-start = (f32[224,128]{1,0:T(8,128)}, f32[224,128]{1,0:T(8,128)S(1)}, u32[]{:S(2)}, u32[]{:S(2)}) collective-permute-start(f32[224,128]{1,0:T(8,128)} %get-tuple-element.26.own_ref), channel_id=1, source_target_pairs={{0,1},{1,2},{2,3},{3,4},{4,5},{5,6},{6,7},{8,9},{9,10},{10,11},{11... | collective-permute-start | bytes 344072 | tf_op jit(solution)/shard_map/ppermute | solution.py:422
  143.2 1.9 %collective-permute-start.1 = (f32[224,128]{1,0:T(8,128)}, f32[224,128]{1,0:T(8,128)S(1)}, u32[]{:S(2)}, u32[]{:S(2)}) collective-permute-start(f32[224,128]{1,0:T(8,128)} %get-tuple-element.26.own_ref), channel_id=1, source_target_pairs={{1,0},{2,1},{3,2},{4,3},{5,4},{6,5},{7,6},{9,8},{10,9},{11,10},{12... | collective-permute-start | bytes 344072 | tf_op jit(solution)/shard_map/ppermute | solution.py:422
  145.1 0.2 collective-permute-done.low_ref
  145.3 4.2 %collective-permute-done.1.high_ref = f32[224,128]{1,0:T(8,128)S(1)} collective-permute-done((f32[224,128]{1,0:T(8,128)}, f32[224,128]{1,0:T(8,128)S(1)}, u32[]{:S(2)}, u32[]{:S(2)}) %collective-permute-start.1) | collective-permute-done | bytes 114720 | tf_op jit(solution)/shard_map/ppermute | solution.py:422
  149.5 0.6 copy-done.3
  150.1 2.9 %make_messages.1 = (f32[3,224,128]{2,1,0:T(8,128)}, f32[3,224,128]{2,1,0:T(8,128)}) custom-call(f32[32,224,128]{2,1,0:T(8,128)} %get-tuple-element.25.block_hbm, f32[224,128]{1,0:T(8,128)} %copy-done.2, f32[224,128]{1,0:T(8,128)} %copy-done.3), custom_call_target="tpu_custom_call" | custom-call | tf_op jit(solution)/shard_map/make_messages/pallas_call | solution.py:293
  153.0 6.7 %collective-permute-start.2 = (f32[3,224,128]{2,1,0:T(8,128)}, f32[3,224,128]{2,1,0:T(8,128)S(1)}, u32[]{:S(2)}, u32[]{:S(2)}) collective-permute-start(f32[3,224,128]{2,1,0:T(8,128)} %get-tuple-element.27), channel_id=1, source_target_pairs={{0,8},{8,16},{16,24},{24,32},{32,40},{40,48},{48,56},{56,64},{64,7... | collective-permute-start | bytes 1032200 | tf_op jit(solution)/shard_map/ppermute | solution.py:422
  159.7 1.9 %collective-permute-start.3 = (f32[3,224,128]{2,1,0:T(8,128)}, f32[3,224,128]{2,1,0:T(8,128)S(1)}, u32[]{:S(2)}, u32[]{:S(2)}) collective-permute-start(f32[3,224,128]{2,1,0:T(8,128)} %get-tuple-element.28), channel_id=1, source_target_pairs={{8,0},{16,8},{24,16},{32,24},{40,32},{48,40},{56,48},{64,56},{72,6... | collective-permute-start | bytes 1032200 | tf_op jit(solution)/shard_map/ppermute | solution.py:422
  161.6 0.6 add_convert_fusion.inside_ref
  162.2 4.6 %collective-permute-done.2.above_ref = f32[3,224,128]{2,1,0:T(8,128)S(1)} collective-permute-done((f32[3,224,128]{2,1,0:T(8,128)}, f32[3,224,128]{2,1,0:T(8,128)S(1)}, u32[]{:S(2)}, u32[]{:S(2)}) %collective-permute-start.2) | collective-permute-done | bytes 344096 | tf_op jit(solution)/shard_map/ppermute | solution.py:422
  166.8 6.1 %collective-permute-done.3.below_ref = f32[3,224,128]{2,1,0:T(8,128)S(1)} collective-permute-done((f32[3,224,128]{2,1,0:T(8,128)}, f32[3,224,128]{2,1,0:T(8,128)S(1)}, u32[]{:S(2)}, u32[]{:S(2)}) %collective-permute-start.3) | collective-permute-done | bytes 344096 | tf_op jit(solution)/shard_map/ppermute | solution.py:422
  172.9 0.8 broadcast_in_dim.28.rate_ref
  173.7 17.5 %diffuse.1 = f32[6976,128]{1,0:T(8,128)} custom-call(f32[4]{0:T(128)} %add_convert_fusion.inside_ref, f32[32,224,128]{2,1,0:T(8,128)} %get-tuple-element.25.block_hbm, f32[3,224,128]{2,1,0:T(8,128)} %copy-done.4, f32[3,224,128]{2,1,0:T(8,128)} %copy-done.5, f32[224,128]{1,0:T(8,128)} %copy-done.2, f32[224,128]{1,0:T(8,128)} %copy-done.3, ...), custom_call_target="tpu_custom_call" | custom-call | tf_op jit(solution)/shard_map/diffuse/pallas_call | solution.py:384
  (30 shorter events, 0.6 us)
Async XLA Ops:
  0.0 73.9 %copy-start = (s32[32,1]{0,1:T(1,128)S(1)}, s32[32,1]{0,1:T(1,128)}, u32[]{:S(2)}) copy-start(s32[32,1]{0,1:T(1,128)} %param.7) | copy-start | bytes 388
  12.3 49.9 %all-to-all-start.1 = ((bf16[16,2,400,128]{3,2,1,0:T(8,128)(2,1)}), bf16[16,2,400,128]{3,2,1,0:T(8,128)(2,1)S(1)}, u32[]{:S(2)}, u32[]{:S(2)}) async-start(bf16[16,2,400,128]{3,2,1,0:T(8,128)(2,1)} %pack_chunk.3), calls=%async_computation.1 | async-start | bytes 6553600 | tf_op jit(solution)/shard_map/all_to_all | solution.py:434
  29.7 40.8 %copy-start.6 = (s32[1,1,16,4]{2,3,1,0:T(4,128)S(1)}, s32[1,1,16,4]{2,3,1,0:T(4,128)}, u32[]{:S(2)}) copy-start(s32[1,1,16,4]{2,3,1,0:T(4,128)} %param.8) | copy-start | bytes 772
  62.2 8.2 %copy-start.1 = (bf16[16,2,400,128]{3,2,1,0:T(8,128)(2,1)}, bf16[16,2,400,128]{3,2,1,0:T(8,128)(2,1)S(1)}, u32[]{:S(2)}) copy-start(bf16[16,2,400,128]{3,2,1,0:T(8,128)(2,1)S(1)} %all-to-all-done.1) | copy-start | bytes 9830404
  62.2 48.2 %all-to-all-start = ((bf16[16,2,400,128]{3,2,1,0:T(8,128)(2,1)}), bf16[16,2,400,128]{3,2,1,0:T(8,128)(2,1)}, u32[]{:S(2)}, u32[]{:S(2)}) async-start(bf16[16,2,400,128]{3,2,1,0:T(8,128)(2,1)} %pack_chunk.2), calls=%async_computation | async-start | bytes 6553600 | tf_op jit(solution)/shard_map/all_to_all | solution.py:434
  132.2 29.5 %copy-start.7 = (f32[218]{0:T(256)S(1)}, f32[218]{0:T(256)}, u32[]{:S(2)}) copy-start(f32[218]{0:T(256)} %param.11) | copy-start | bytes 2620
  132.2 13.1 %collective-permute-start = (f32[224,128]{1,0:T(8,128)}, f32[224,128]{1,0:T(8,128)S(1)}, u32[]{:S(2)}, u32[]{:S(2)}) collective-permute-start(f32[224,128]{1,0:T(8,128)} %get-tuple-element.26.own_ref), channel_id=1, source_target_pairs={{0,1},{1,2},{2,3},{3,4},{4,5},{5,6},{6,7},{8,9},{9,10},{10,11},{11... | collective-permute-start | bytes 344072 | tf_op jit(solution)/shard_map/ppermute | solution.py:422
  143.2 6.3 %collective-permute-start.1 = (f32[224,128]{1,0:T(8,128)}, f32[224,128]{1,0:T(8,128)S(1)}, u32[]{:S(2)}, u32[]{:S(2)}) collective-permute-start(f32[224,128]{1,0:T(8,128)} %get-tuple-element.26.own_ref), channel_id=1, source_target_pairs={{1,0},{2,1},{3,2},{4,3},{5,4},{6,5},{7,6},{9,8},{10,9},{11,10},{12... | collective-permute-start | bytes 344072 | tf_op jit(solution)/shard_map/ppermute | solution.py:422
  145.3 4.2 %copy-start.2 = (f32[224,128]{1,0:T(8,128)}, f32[224,128]{1,0:T(8,128)S(1)}, u32[]{:S(2)}) copy-start(f32[224,128]{1,0:T(8,128)S(1)} %collective-permute-done.low_ref) | copy-start | bytes 344068
  149.5 0.6 copy-start.3
  153.0 13.8 %collective-permute-start.2 = (f32[3,224,128]{2,1,0:T(8,128)}, f32[3,224,128]{2,1,0:T(8,128)S(1)}, u32[]{:S(2)}, u32[]{:S(2)}) collective-permute-start(f32[3,224,128]{2,1,0:T(8,128)} %get-tuple-element.27), channel_id=1, source_target_pairs={{0,8},{8,16},{16,24},{24,32},{32,40},{40,48},{48,56},{56,64},{64,7... | collective-permute-start | bytes 1032200 | tf_op jit(solution)/shard_map/ppermute | solution.py:422
  159.7 13.3 %collective-permute-start.3 = (f32[3,224,128]{2,1,0:T(8,128)}, f32[3,224,128]{2,1,0:T(8,128)S(1)}, u32[]{:S(2)}, u32[]{:S(2)}) collective-permute-start(f32[3,224,128]{2,1,0:T(8,128)} %get-tuple-element.28), channel_id=1, source_target_pairs={{8,0},{16,8},{24,16},{32,24},{40,32},{48,40},{56,48},{64,56},{72,6... | collective-permute-start | bytes 1032200 | tf_op jit(solution)/shard_map/ppermute | solution.py:422
  166.8 6.9 %copy-start.4 = (f32[3,224,128]{2,1,0:T(8,128)}, f32[3,224,128]{2,1,0:T(8,128)S(1)}, u32[]{:S(2)}) copy-start(f32[3,224,128]{2,1,0:T(8,128)S(1)} %collective-permute-done.2.above_ref) | copy-start | bytes 1032196
  172.9 0.8 copy-start.5

commit v2 on v0

v2 whole, which is shorter than its diff:
```python
import functools

import jax
import numpy as np
import jax.numpy as jnp
from jax import lax
from jax.experimental import pallas as pl
from jax.experimental.pallas import tpu as pltpu
from jax.sharding import PartitionSpec as P

S = 218
SR = 224
SP = 256
BL = 64
NB = 4
PACK = 400
LANES = 128
EPSILON = 1e-06
GROUP = 8
SLOTS = 4
CHUNKS = ((0, 3), (3, 1))
PACK_BOXES = 4
SPECIES = 56
WIDE_VMEM = 61 * 1024 * 1024


def lane_iota(rows):
    return lax.broadcasted_iota(jnp.int32, (rows, LANES), 1)


def make_plan(table, counts):
    slots, boxes = table.shape
    tiles = counts.shape[1]
    size = float(LANES)
    filler = jnp.full((slots, LANES - boxes), -1.0, jnp.float32)
    spread = jnp.concatenate([table.astype(jnp.float32), filler], axis=1)
    counts = jnp.concatenate(
        [counts.astype(jnp.float32), jnp.zeros((1, LANES - tiles), jnp.float32)], axis=1
    )
    lane = lane_iota(LANES).astype(jnp.float32)
    item = lax.broadcasted_iota(jnp.int32, (LANES, LANES), 0).astype(jnp.float32)
    row = jnp.full((1, LANES), -1.0, jnp.float32)
    for slot in range(slots):
        part = pltpu.roll(spread, slot * boxes, 1)[slot : slot + 1] if slot else spread[0:1]
        here = (lane_iota(1) >= slot * boxes) & (lane_iota(1) < (slot + 1) * boxes)
        row = jnp.where(here, part, row)
    tile = jnp.transpose(jnp.broadcast_to(row, (LANES, LANES)))
    turns = jnp.sum(jnp.where(tile == lane, counts, 0.0), axis=1, keepdims=True)
    turns = jnp.broadcast_to(turns, (LANES, LANES))
    live = tile >= 0.0
    early_size = CHUNKS[0][1] * boxes
    early = live & (item < early_size)
    weight = (size - turns) * size + item

    def rank(key):
        smaller = jnp.where(jnp.transpose(key) < key, 1.0, 0.0)
        return jnp.broadcast_to(jnp.sum(smaller, axis=1, keepdims=True), (LANES, LANES))

    late = 4.0 * size * size
    begun = jnp.sum(jnp.where(early, 1.0, 0.0), axis=0, keepdims=True)
    begun = jnp.floor(begun * (1.0 / GROUP)) * GROUP
    chosen = early & (rank(jnp.where(early, weight, late + item)) < begun)
    place = rank(weight + jnp.where(chosen, 0.0, jnp.where(live, late, 2.0 * late)))
    slot_of = jnp.floor(item * (1.0 / boxes))
    box_of = item - slot_of * boxes
    width = float(CHUNKS[0][1])
    source = jnp.where(item < early_size, box_of * width + slot_of, item)
    rows = [
        jnp.sum(jnp.where(place == lane, value, 0.0), axis=0, keepdims=True)
        for value in (source, tile, turns)
    ]
    rows += [begun, jnp.zeros((4, LANES), jnp.float32)]
    return jnp.concatenate(rows, axis=0).astype(jnp.int32)


def pack_kernel(pattern_ref, table_ref, counts_ref, jac_ref, plan_ref, *out_refs):
    @pl.when(pl.program_id(0) == 0)
    def _():
        plan_ref[...] = make_plan(table_ref[...], counts_ref[...])

    low_half = lane_iota(1) < BL
    half_rows = SR // 2
    tail = SR - (NB - 1) * BL
    inside = lax.broadcasted_iota(jnp.int32, (tail, LANES), 0) < S - (NB - 1) * BL
    inside = inside.astype(jnp.float32).astype(jnp.bfloat16)
    middle_lane = lane_iota(half_rows)
    edge_lane = lane_iota(BL)

    def one_box(inner, carry):
        box = pl.program_id(0) * PACK_BOXES + inner
        for slot in range(SLOTS):
            chunk = next(k for k, (at, n) in enumerate(CHUNKS) if at <= slot < at + n)
            put = functools.partial(out_refs[chunk].__setitem__)
            place = slot - CHUNKS[chunk][0]
            held = box * SLOTS + slot
            right = []
            for p in range(NB):
                rows = min(SR, (p + 1) * BL) - p * BL
                parts = []
                for half in range(2):
                    mask = jnp.where(
                        low_half,
                        pattern_ref[p, 2 * half, held].astype(jnp.float32),
                        pattern_ref[p, 2 * half + 1, held].astype(jnp.float32),
                    ).astype(jnp.bfloat16)
                    value = (
                        jac_ref[inner, slot, p * BL : p * BL + rows, half * LANES : (half + 1) * LANES]
                        * mask
                    )
                    parts.append(value * inside if p == NB - 1 else value)
                put((inner, place, slice(p * BL, p * BL + rows), slice(None)), parts[0])
                right.append(parts[1])
            upper = jnp.concatenate([right[0], right[1][: half_rows - BL]], axis=0)
            lower = jnp.concatenate([right[1][half_rows - BL :], right[2], right[3]], axis=0)
            middle = jnp.where(middle_lane < BL, upper, pltpu.roll(lower, BL, 1))
            put((inner, place, slice(SR, SR + half_rows), slice(None)), middle)
            last = jnp.concatenate([right[3], jnp.zeros((BL - tail, LANES), jnp.bfloat16)], axis=0)
            edge = jnp.where(
                edge_lane < 64,
                jnp.where(edge_lane < 32, pltpu.roll(right[0], 64, 1), pltpu.roll(right[1], 96, 1)),
                jnp.where(edge_lane < 96, right[2], pltpu.roll(last, 32, 1)),
            )
            put((inner, place, slice(SR + half_rows, PACK), slice(None)), edge)
        return carry

    lax.fori_loop(0, PACK_BOXES, one_box, 0)


def pack_all(jacobian, pattern, table, counts):
    boxes = jacobian.shape[0]
    return pl.pallas_call(
        pack_kernel,
        grid=(boxes // PACK_BOXES,),
        in_specs=[
            pl.BlockSpec(memory_space=pltpu.SMEM),
            pl.BlockSpec(table.shape, lambda b: (0, 0)),
            pl.BlockSpec(counts.shape, lambda b: (0, 0)),
            pl.BlockSpec((PACK_BOXES, SLOTS, SR, SP), lambda b: (b, 0, 0, 0)),
        ],
        out_specs=[pl.BlockSpec((8, LANES), lambda b: (0, 0))]
        + [
            pl.BlockSpec((PACK_BOXES, n, PACK, LANES), lambda b: (b, 0, 0, 0)) for _, n in CHUNKS
        ],
        out_shape=[jax.ShapeDtypeStruct((8, LANES), jnp.int32)]
        + [
            jax.ShapeDtypeStruct((boxes, n, PACK, LANES), jnp.bfloat16) for _, n in CHUNKS
        ],
        compiler_params=pltpu.CompilerParams(vmem_limit_bytes=WIDE_VMEM),
        name="pack_all",
    )(pattern, table, counts, jacobian)


def unpack(packed_ref, item, dense_ref):
    half_rows = SR // 2
    dense_ref[:, 0:LANES] = packed_ref[item, pl.ds(0, SR), :]
    middle = packed_ref[item, pl.ds(SR, half_rows), :]
    edge = packed_ref[item, pl.ds(SR + half_rows, BL), :]
    high = pltpu.roll(middle, BL, 1)

    def put(row, rows, low, rest):
        dense_ref[pl.ds(row, rows), LANES:SP] = jnp.where(lane_iota(rows) < BL, low, rest)

    put(0, 64, middle[0:64], pltpu.roll(edge, 64, 1))
    shifted = pltpu.roll(edge, 32, 1)
    put(64, 48, middle[64:112], shifted[0:48])
    put(112, 16, high[0:16], shifted[48:64])
    put(128, 64, high[16:80], edge)
    put(192, 32, high[80:112], pltpu.roll(edge[0:32], 96, 1))


def solve_kernel(chunk, *refs):
    if chunk == 0:
        plan_ref, state_hbm, packed_hbm, out_hbm, edge_ref = refs[:5]
        scratch = refs[5:]
    else:
        plan_ref, state_hbm, packed_hbm, second_hbm, _, edge_in, out_hbm, edge_ref = refs[:8]
        scratch = refs[8:]
    packed, state, outgoing, arrived, state_sem, sent = scratch[:6]
    dense, right, left_over, mapped, guess, sums = (
        scratch[6 + GROUP * kind : 6 + GROUP * (kind + 1)] for kind in range(6)
    )
    tiles = state.shape[0]
    begun = plan_ref[3, 0]
    base = 0 if chunk == 0 else begun
    groups = (begun if chunk == 0 else tiles - begun) // GROUP
    state_copy = pltpu.make_async_copy(state_hbm, state, state_sem)
    state_copy.start()

    def fetch(place, origin, at):
        return pltpu.make_async_copy(origin.at[at], packed.at[place], arrived.at[place])

    def start_fetch(place, carry):
        at = plan_ref[0, base + place]
        if chunk == 0:
            fetch(place, packed_hbm, at).start()
        else:
            early = packed_hbm.shape[0]

            @pl.when(at < early)
            def _():
                fetch(place, packed_hbm, at).start()

            @pl.when(at >= early)
            def _():
                fetch(place, second_hbm, at - early).start()

        return carry

    lax.fori_loop(0, groups * GROUP, start_fetch, 0)
    for member in range(GROUP):
        right[member][...] = jnp.zeros_like(right[member])
    if chunk == 0:
        edge_ref[...] = jnp.zeros_like(edge_ref)
    else:
        edge_ref[...] = edge_in[...]
    state_copy.wait()
    edge_lane = lane_iota(SR) // 4

    def send(buffer, member, tile):
        return pltpu.make_async_copy(
            outgoing.at[buffer, member], out_hbm.at[tile], sent.at[buffer, member]
        )

    def drain(group_no):
        for member in range(GROUP):
            send(group_no % 2, member, plan_ref[1, base + group_no * GROUP + member]).wait()

    def split(member, row, rows, remainder):
        high = remainder.astype(jnp.bfloat16)
        span = slice(row, row + rows)
        right[member][span, 0:LANES] = high
        right[member][span, LANES:SP] = (remainder - high.astype(jnp.float32)).astype(
            jnp.bfloat16
        )

    def multiply(member):
        return jnp.dot(
            dense[member][...], right[member][...], preferred_element_type=jnp.float32
        )

    def measure(member, product):
        above = jnp.zeros((8, LANES), jnp.float32)
        below = jnp.zeros((8, LANES), jnp.float32)
        for row in range(0, SR, 8):
            span = slice(row, row + 8)
            remainder = left_over[member][span, :]
            value = remainder - (product[span, 0:LANES] + product[span, LANES:SP])
            mapped[member][span, :] = value
            above = above + remainder * value
            below = below + value * value
        return above, below

    def move(member, above, below, active):
        above = jnp.sum(above, axis=0, keepdims=True)
        below = jnp.sum(below, axis=0, keepdims=True) + EPSILON
        step = jnp.where(active, above / below, 0.0)
        for row in range(0, SR, 16):
            span = slice(row, row + 16)
            remainder = left_over[member][span, :]
            guess[member][span, :] += step * remainder
            remainder = remainder - step * mapped[member][span, :]
            left_over[member][span, :] = remainder
            split(member, row, 16, remainder)

    def keep_sums(member, above, below):
        sums[member][0:8, :] = above
        sums[member][8:16, :] = below

    def one_group(group_no, carry):
        buffer = group_no % 2
        places = [group_no * GROUP + member for member in range(GROUP)]
        chosen = [plan_ref[1, base + place] for place in places]
        counts = [plan_ref[2, base + place] for place in places]

        for member in range(GROUP):
            fetch(places[member], packed_hbm, 0).wait()
        for member in range(GROUP):
            unpack(packed, places[member], dense[member])
            start_value = state[chosen[member]]
            right[member][0:SR, 0:LANES] = start_value
            guess[member][...] = start_value.astype(jnp.float32)
        for member in range(GROUP):
            remainder = jnp.dot(
                dense[member][...],
                right[member][:, 0:LANES],
                preferred_element_type=jnp.float32,
            )
            left_over[member][...] = remainder
            split(member, 0, SR, remainder)

        half = GROUP // 2
        for member in range(half, GROUP):
            keep_sums(member, *measure(member, multiply(member)))

        def advance(turn_no, inner):
            for one, other in zip(range(half), range(half, GROUP)):
                product = multiply(one)
                move(other, sums[other][0:8, :], sums[other][8:16, :], turn_no < counts[other])
                next_product = multiply(other)
                move(one, *measure(one, product), turn_no < counts[one])
                keep_sums(other, *measure(other, next_product))
            return inner

        lax.fori_loop(0, functools.reduce(jnp.maximum, counts), advance, 0)

        @pl.when(group_no >= 2)
        def _():
            drain(group_no - 2)

        for member in range(GROUP):
            result = guess[member][...]
            outgoing[buffer, member] = result
            tile = chosen[member]
            edge_ref[...] = jnp.where(
                edge_lane == tile, pltpu.roll(result, (4 * tile + 2) % LANES, 1), edge_ref[...]
            )
            send(buffer, member, tile).start()
        return carry

    lax.fori_loop(0, groups, one_group, 0)

    for back in range(2):
        @pl.when(groups > back)
        def _():
            drain(groups - 1 - back)


def solve_chunk(chunk, plan, state, packed, reacted, edge):
    tiles = state.shape[0]
    out_shape = (
        jax.ShapeDtypeStruct((tiles, SR, LANES), jnp.float32),
        jax.ShapeDtypeStruct((SR, LANES), jnp.float32),
    )
    anywhere = pl.BlockSpec(memory_space=pl.ANY)
    vmem = pl.BlockSpec(memory_space=pltpu.VMEM)
    in_specs = [pl.BlockSpec(memory_space=pltpu.SMEM), anywhere]
    in_specs += [anywhere] * (chunk + 1)
    operands = [plan, state, *packed[: chunk + 1]]
    aliases = {}
    if chunk:
        in_specs += [anywhere, vmem]
        operands += [reacted, edge]
        aliases = {4: 0}
    tile_values = pltpu.VMEM((SR, LANES), jnp.float32)
    return pl.pallas_call(
        functools.partial(solve_kernel, chunk),
        in_specs=in_specs,
        out_specs=(anywhere, vmem),
        out_shape=out_shape,
        input_output_aliases=aliases,
        scratch_shapes=[
            pltpu.VMEM((tiles, PACK, LANES), jnp.bfloat16),
            pltpu.VMEM((tiles, SR, LANES), jnp.bfloat16),
            pltpu.VMEM((2, GROUP, SR, LANES), jnp.float32),
            pltpu.SemaphoreType.DMA((tiles,)),
            pltpu.SemaphoreType.DMA,
            pltpu.SemaphoreType.DMA((2, GROUP)),
        ]
        + [pltpu.VMEM((SR, SP), jnp.bfloat16)] * GROUP
        + [pltpu.VMEM((SP, SP), jnp.bfloat16)] * GROUP
        + [tile_values] * (3 * GROUP)
        + [pltpu.VMEM((16, LANES), jnp.float32)] * GROUP,
        compiler_params=pltpu.CompilerParams(vmem_limit_bytes=WIDE_VMEM),
        cost_estimate=pl.CostEstimate(
            flops=16 * 300_000_000, bytes_accessed=16 * 200000, transcendentals=0
        ),
        name="solve_chunk",
    )(*operands)


def message_kernel(bottom_ref, top_ref, low_ref, high_ref, down_ref, up_ref):
    tiles = LANES // 4
    down_ref[0:2] = bottom_ref[...].astype(jnp.bfloat16)
    up_ref[0:2] = top_ref[...].astype(jnp.bfloat16)
    lanes = lane_iota(SR)
    for row, out_ref in ((tiles - 1, down_ref), (0, up_ref)):
        out_ref[2] = jnp.where(
            lanes == 0,
            pltpu.roll(low_ref[...], (-(4 * row + 1)) % LANES, 1),
            pltpu.roll(high_ref[...], (-(4 * row + 3)) % LANES, 1),
        ).astype(jnp.bfloat16)


def make_messages(block, low, high):
    tiles = block.shape[0]
    shape = jax.ShapeDtypeStruct((3, SR, LANES), jnp.bfloat16)
    edge = pl.BlockSpec((SR, LANES), lambda i: (0, 0))
    message = pl.BlockSpec((3, SR, LANES), lambda i: (0, 0, 0))
    return pl.pallas_call(
        message_kernel,
        grid=(1,),
        in_specs=[
            pl.BlockSpec((2, SR, LANES), lambda i: (tiles // 2 - 1, 0, 0)),
            pl.BlockSpec((2, SR, LANES), lambda i: (0, 0, 0)),
            edge,
            edge,
        ],
        out_specs=(message, message),
        out_shape=(shape, shape),
        compiler_params=pltpu.CompilerParams(vmem_limit_bytes=WIDE_VMEM),
        name="make_messages",
    )(block, block, low, high)


def beside(value, lanes):
    return jnp.where(lanes == 0, 0.0, pltpu.roll(value, 1, 1)) + jnp.where(
        lanes == LANES - 1, 0.0, pltpu.roll(value, LANES - 1, 1)
    )


def inner_kernel(tiles, block_ref, rate_ref, both_ref, out_ref):
    zero = jnp.zeros((1, 8, LANES), jnp.float32)

    def around(value, by):
        gap = jnp.concatenate([zero] * by, axis=0)
        return jnp.concatenate([gap, value[: tiles - by]], axis=0) + jnp.concatenate(
            [value[by:], gap], axis=0
        )

    for number in range(SPECIES // 8):
        span = slice(number * 8, number * 8 + 8)
        rate = rate_ref[span, :]
        keep = 1.0 - 4.0 * rate
        square = rate * rate
        cells = block_ref[:, span, :]
        flat = cells.reshape(tiles * 8, LANES)
        high = flat.astype(jnp.bfloat16)
        low = (flat - high.astype(jnp.float32)).astype(jnp.bfloat16)
        product = jnp.dot(
            jnp.concatenate([high, low], axis=1), both_ref[...], preferred_element_type=jnp.float32
        )
        once = product[:, 0:LANES].reshape(tiles, 8, LANES)
        twice = product[:, LANES:].reshape(tiles, 8, LANES)
        near = (2.0 * keep * rate) * (around(cells, 1) + once)
        sides = around(once, 1)
        far = square * ((around(cells, 2) + twice) + (sides + sides))
        own = keep * keep + 2.0 * square
        end = keep * keep + square
        value = near + far
        out_ref[1 : tiles - 1, span, :] = value[1 : tiles - 1] + own * cells[1 : tiles - 1]
        out_ref[0, span, :] = value[0] + end * cells[0]
        out_ref[tiles - 1, span, :] = value[tiles - 1] + end * cells[tiles - 1]


def diffuse_inside(block, rate):
    tiles = block.shape[0]
    cells = pl.BlockSpec((tiles, SPECIES, LANES), lambda g: (0, g, 0))
    place = np.arange(LANES)
    next_to = (np.abs(place[:, None] - place[None, :]) == 1).astype(np.float32)
    both = np.concatenate([next_to, next_to @ next_to], axis=1)
    both = jnp.asarray(np.concatenate([both, both], axis=0), jnp.bfloat16)
    return pl.pallas_call(
        functools.partial(inner_kernel, tiles),
        grid=(SR // SPECIES,),
        in_specs=[
            cells,
            pl.BlockSpec((SPECIES, LANES), lambda g: (g, 0)),
            pl.BlockSpec((2 * LANES, 2 * LANES), lambda g: (0, 0)),
        ],
        out_specs=cells,
        out_shape=jax.ShapeDtypeStruct(block.shape, jnp.float32),
        compiler_params=pltpu.CompilerParams(vmem_limit_bytes=WIDE_VMEM),
        cost_estimate=pl.CostEstimate(
            flops=tiles * SR * LANES * 20, bytes_accessed=8 * block.size, transcendentals=0
        ),
        name="diffuse_inside",
    )(block, rate, both)


def border_kernel(tiles, inside_ref, inner_ref, top_ref, bottom_ref, above_ref, below_ref,
                  low_ref, high_ref, own_ref, rate_ref, out_ref):
    lanes = lane_iota(8)
    column = lanes % 4
    has_above, has_below = inside_ref[0], inside_ref[1]
    has_side = jnp.where(column < 2, inside_ref[2], inside_ref[3])
    near_edge = (lanes < 2) | (lanes >= LANES - 2)

    def slab(number):
        span = slice(number * 8, number * 8 + 8)
        overall = pl.program_id(0) * (SPECIES // 8) + number
        wide = pl.ds(pl.multiple_of(overall // 2 * 16, 16), 16)

        def read(ref, row):
            both = ref[row, wide, :].astype(jnp.float32)
            return jnp.where(overall % 2 == 0, both[0:8], both[8:16])

        rate = rate_ref[span, :]
        keep = 1.0 - 4.0 * rate
        own = own_ref[span, :]
        ghost = jnp.where(column < 2, low_ref[span, :], high_ref[span, :])

        def rows_beside(near, far, inner, corner, exists):
            left = jnp.where(lanes == 0, corner, pltpu.roll(near, 1, 1))
            right = jnp.where(lanes == LANES - 1, corner, pltpu.roll(near, LANES - 1, 1))
            later = (keep * near + rate * ((far + inner) + (left + right))) * exists
            first = rate * near
            outer = keep * first + rate * (beside(first, lanes) + later)
            return outer, rate * first

        corner_above, corner_below = read(above_ref, 2), read(below_ref, 2)
        row_terms = {}
        row_terms[0], row_terms[1] = rows_beside(
            read(above_ref, 1), read(above_ref, 0), top_ref[0, span, :], corner_above, has_above
        )
        row_terms[tiles - 1], row_terms[tiles - 2] = rows_beside(
            read(below_ref, 0), read(below_ref, 1), bottom_ref[0, span, :], corner_below, has_below
        )

        up = pltpu.roll(ghost, 4, 1)
        up = jnp.where(lanes == 1, pltpu.roll(corner_above, 1, 1), up)
        up = jnp.where(lanes == 2, pltpu.roll(corner_above, 3, 1), up)
        down = pltpu.roll(ghost, LANES - 4, 1)
        down = jnp.where(lanes == LANES - 3, pltpu.roll(corner_below, LANES - 3, 1), down)
        down = jnp.where(lanes == LANES - 2, pltpu.roll(corner_below, LANES - 1, 1), down)
        side = jnp.where(
            column == 1,
            pltpu.roll(own, LANES - 1, 1) + pltpu.roll(ghost, 1, 1),
            pltpu.roll(own, 1, 1) + pltpu.roll(ghost, LANES - 1, 1),
        )
        later = (keep * ghost + rate * ((up + down) + side)) * has_side
        first = rate * ghost
        first_up = jnp.where(lanes < 4, 0.0, pltpu.roll(first, 4, 1))
        first_down = jnp.where(lanes >= LANES - 4, 0.0, pltpu.roll(first, LANES - 4, 1))
        outer = keep * first + rate * ((first_up + first_down) + later)
        second = rate * first
        terms = jnp.where(
            column < 2,
            jnp.where(column == 0, pltpu.roll(second, LANES - 2, 1), pltpu.roll(outer, LANES - 1, 1)),
            jnp.where(column == 2, pltpu.roll(outer, 1, 1), pltpu.roll(second, 2, 1)),
        )
        values = []
        for row in range(tiles):
            value = inner_ref[row, span, :] + jnp.where(
                near_edge, pltpu.roll(terms, (-(4 * row + 2)) % LANES, 1), 0.0
            )
            if row in row_terms:
                value = value + row_terms[row]
            values.append(value)
        out_ref[span, :, :] = jnp.swapaxes(jnp.stack(values, axis=0), 0, 1)

    for number in range(SPECIES // 8):
        slab(number)


def add_borders(inside, inner, block, above, below, low, high, own, rate):
    tiles = block.shape[0]
    message = pl.BlockSpec((3, SR, LANES), lambda g: (0, 0, 0))
    edge = pl.BlockSpec((SPECIES, LANES), lambda g: (g, 0))
    return pl.pallas_call(
        functools.partial(border_kernel, tiles),
        grid=(SR // SPECIES,),
        in_specs=[
            pl.BlockSpec(memory_space=pltpu.SMEM),
            pl.BlockSpec((tiles, SPECIES, LANES), lambda g: (0, g, 0)),
            pl.BlockSpec((1, SPECIES, LANES), lambda g: (0, g, 0)),
            pl.BlockSpec((1, SPECIES, LANES), lambda g: (tiles - 1, g, 0)),
            message,
            message,
            edge,
            edge,
            edge,
            edge,
        ],
        out_specs=pl.BlockSpec((SPECIES, tiles, LANES), lambda g: (g, 0, 0)),
        out_shape=jax.ShapeDtypeStruct((S, tiles, LANES), jnp.float32),
        compiler_params=pltpu.CompilerParams(vmem_limit_bytes=WIDE_VMEM),
        name="add_borders",
    )(inside, inner, block, block, above, below, low, high, own, rate)


def shifted(value, axis, by):
    count = lax.axis_size(axis)
    pairs = [(i, i + by) for i in range(count) if 0 <= i + by < count]
    return lax.ppermute(value, axis, pairs)


def on_device(species_state, stiffness, send_list, jacobian, pattern, diffusivity):
    boxes = lax.axis_size("box")
    tiles = species_state.shape[0]
    slots = jacobian.shape[0] // boxes
    by_box = jacobian.reshape(boxes, slots, SP, SP)
    counts = stiffness.reshape(1, tiles)
    table = send_list.transpose(0, 1, 3, 2).reshape(slots, boxes)
    place = lax.axis_index("box"), lax.axis_index("bal")
    inside = jnp.stack(
        [
            place[0] > 0,
            place[0] < boxes - 1,
            place[1] > 0,
            place[1] < lax.axis_size("bal") - 1,
        ]
    ).astype(jnp.float32)
    rate = jnp.broadcast_to(jnp.pad(diffusivity, (0, SR - S))[:, None], (SR, LANES))
    state = jnp.pad(species_state, ((0, 0), (0, SR - S), (0, 0)))
    by_block = pattern.transpose(1, 2, 3, 0).reshape(NB, NB, boxes * slots)
    plan, first, second = pack_all(by_box, by_block, table, counts)
    first, second, plan, inside, rate, state = lax.optimization_barrier(
        (first, second, plan, inside, rate, state)
    )

    def exchange(packed):
        arrived = lax.all_to_all(packed, "box", split_axis=0, concat_axis=0, tiled=True)
        return arrived.reshape(-1, PACK, LANES)

    first = exchange(first)
    first, second, plan, inside, rate, state = lax.optimization_barrier(
        (first, second, plan, inside, rate, state)
    )
    second = exchange(second)
    reacted, edge = solve_chunk(0, plan, state, (first, second), None, None)
    reacted, edge = solve_chunk(1, plan, state, (first, second), reacted, edge)

    low = shifted(edge, "bal", 1)
    high = shifted(edge, "bal", -1)
    down, up = make_messages(reacted, low, high)
    above = shifted(down, "box", 1)
    below = shifted(up, "box", -1)
    inner = diffuse_inside(reacted, rate)
    field = add_borders(inside, inner, reacted, above, below, low, high, edge, rate)
    return field.transpose(1, 0, 2)


def solution(mesh):
    in_specs = (
        P("box", None, "bal"),
        P("box", "bal"),
        P("box", "bal", None, None),
        P("box", "bal", None, None),
        P("box", "bal", None, None),
        P(),
    )
    return jax.shard_map(
        on_device,
        mesh=mesh,
        in_specs=in_specs,
        out_specs=P("box", None, "bal"),
        check_vma=False,
    )
```

time: 744 us -> 158 us (0.21)
  the two profiles are of different devices: /device:TPU:3 before, /device:TPU:66 now
where the time goes in v2:
time: 158 us
  blocking collectives  65.1 us (41%)
  Pallas kernels  62.2 us (39%)
  starting transfers between devices  17.5 us (11%)
  local copies, waits for them, and re-layouts  8.17 us (5%)
  waiting for transfers between devices  3.91 us (2%)
    all_to_all x1, blocking collectives, exchange(): lax.all_to_all(packed, 'box', split_axis=0, concat_axis=0, tiled=True)  65.1 us
    pallas_call x2, Pallas kernels, solve_chunk(): pl.pallas_call(functools.partial(solve_kernel, chunk), in_specs=in_specs,...  39.5 us
    ppermute x4, starting transfers between devices, shifted(): return lax.ppermute(value, axis, pairs)  12.3 us
    pallas_call x1, Pallas kernels, pack_all(): pl.pallas_call(pack_kernel, grid=(boxes // PACK_BOXES,), in_specs=[pl.Blo...  8.24 us
    pallas_call x1, Pallas kernels, add_borders(): pl.pallas_call(functools.partial(border_kernel, tiles), grid=(SR // SPECI...  7 us
    pallas_call x1, Pallas kernels, diffuse_inside(): pl.pallas_call(functools.partial(inner_kernel, tiles), grid=(SR // SPECIE...  5.52 us
    unnamed x11, local copies, waits for them, and re-layouts  5.38 us
    all_to_all x1, starting transfers between devices, exchange(): lax.all_to_all(packed, 'box', split_axis=0, concat_axis=0, tiled=True)  5.22 us
  transfers between devices with their start and end apart: 5, of which 2 were waited for; matrix products, arithmetic and copies ran while one was open for 0% of the time, Pallas kernels for 20%

profile of v2, /device:TPU:66, one launch (start us, length us, event | category | flops | bytes accessed | tf_op | source)
XLA Modules:
  0.0 157.6 jit_solution(18394160409080389515)
XLA Ops:
  0.0 2.2 %copy.11 = bf16[32,218,128]{2,1,0:T(8,128)(2,1)S(1)} copy(bf16[32,218,128]{2,0,1:T(8,128)(2,1)} %param.7) | data formatting | bytes 3571712 | tf_op args[0]
  2.2 0.7 pad.8
  2.9 1.4 pad.9.refs_1_
  4.2 0.6 add_convert_fusion.inside_ref
  4.9 8.2 %pack_all.1 = (s32[8,128]{1,0:T(8,128)}, bf16[16,3,400,128]{3,2,1,0:T(8,128)(2,1)}, bf16[16,1,400,128]{3,2,1,0:T(8,128)(2,1)}) custom-call(s32[4,4,64]{2,1,0:T(4,128)} %bitcast.19, s32[4,16]{1,0:T(4,128)} %bitcast.20, s32[1,32]{1,0:T(1,128)} %bitcast.21, bf16[16,4,256,256]{3,2,1,0:T(8,128)(2,1)} %bitcast.15), custom_call_target="tpu_custom_call" | custom-call | tf_op jit(solution)/shard_map/pack_all/pallas_call | solution.py:131
  13.1 0.7 broadcast_in_dim.2.rate_ref
  13.8 65.1 %all_to_all.10 = bf16[16,3,400,128]{3,2,1,0:T(8,128)(2,1)} all-to-all(bf16[16,3,400,128]{3,2,1,0:T(8,128)(2,1)} %get-tuple-element.29), channel_id=1, replica_groups=mesh['box'=16,'bal'=8] {'box'}, dimensions={0} | all-to-all | bytes 9830400 | tf_op jit(solution)/shard_map/all_to_all | solution.py:602
  78.9 5.2 %all-to-all-start.1 = ((bf16[16,1,400,128]{3,2,1,0:T(8,128)(2,1)}), bf16[16,1,400,128]{3,2,1,0:T(8,128)(2,1)S(1)}, u32[]{:S(2)}, u32[]{:S(2)}) async-start(bf16[16,1,400,128]{3,2,1,0:T(8,128)(2,1)} %get-tuple-element.39), calls=%async_computation.1 | async-start | bytes 3276800 | tf_op jit(solution)/shard_map/all_to_all | solution.py:602
  84.2 26.4 %solve_chunk.2 = (f32[32,224,128]{2,1,0:T(8,128)}, f32[224,128]{1,0:T(8,128)}) custom-call(s32[8,128]{1,0:T(8,128)} %get-tuple-element.36.refs_0_, bf16[32,224,128]{2,1,0:T(8,128)(2,1)} %pad.9.refs_1_, bf16[48,400,128]{2,1,0:T(8,128)(2,1)} %bitcast.16), custom_call_target="tpu_custom_call" | custom-call | flops 4800000000 | bytes 3200000 | tf_op jit(solution)/shard_map/solve_chunk/pallas_call | solution.py:345
  110.6 0.0 all-to-all-done.1
  110.6 0.0 copy-start
  110.6 1.2 copy-done
  111.8 13.0 %solve_chunk.3 = (f32[32,224,128]{2,1,0:T(8,128)}, f32[224,128]{1,0:T(8,128)}) custom-call(s32[8,128]{1,0:T(8,128)} %get-tuple-element.36.refs_0_, bf16[32,224,128]{2,1,0:T(8,128)(2,1)} %pad.9.refs_1_, bf16[48,400,128]{2,1,0:T(8,128)(2,1)} %bitcast.17, bf16[16,400,128]{2,1,0:T(8,128)(2,1)} %bitcast.18, ...), custom_call_target="tpu_custom_call", output_to_operand_aliasing={{0}: (4, {})} | custom-call | flops 4800000000 | bytes 3200000 | tf_op jit(solution)/shard_map/solve_chunk/pallas_call | solution.py:345
  124.9 1.9 %collective-permute-start.1 = (f32[224,128]{1,0:T(8,128)}, f32[224,128]{1,0:T(8,128)S(1)}, u32[]{:S(2)}, u32[]{:S(2)}) collective-permute-start(f32[224,128]{1,0:T(8,128)} %get-tuple-element.44.own_ref), channel_id=1, source_target_pairs={{1,0},{2,1},{3,2},{4,3},{5,4},{6,5},{7,6},{9,8},{10,9},{11,10},{12... | collective-permute-start | bytes 344072 | tf_op jit(solution)/shard_map/ppermute | solution.py:574
  126.8 2.4 %collective-permute-start = (f32[224,128]{1,0:T(8,128)}, f32[224,128]{1,0:T(8,128)S(1)}, u32[]{:S(2)}, u32[]{:S(2)}) collective-permute-start(f32[224,128]{1,0:T(8,128)} %get-tuple-element.44.own_ref), channel_id=1, source_target_pairs={{0,1},{1,2},{2,3},{3,4},{4,5},{5,6},{6,7},{8,9},{9,10},{10,11},{11... | collective-permute-start | bytes 344072 | tf_op jit(solution)/shard_map/ppermute | solution.py:574
  129.2 0.2 collective-permute-done.1.high_ref
  129.5 0.0 copy-start.1
  129.5 3.7 %collective-permute-done.low_ref = f32[224,128]{1,0:T(8,128)S(1)} collective-permute-done((f32[224,128]{1,0:T(8,128)}, f32[224,128]{1,0:T(8,128)S(1)}, u32[]{:S(2)}, u32[]{:S(2)}) %collective-permute-start) | collective-permute-done | bytes 114720 | tf_op jit(solution)/shard_map/ppermute | solution.py:574
  133.1 0.0 copy-start.2
  133.1 0.0 copy-done.1
  133.1 0.6 copy-done.2
  133.8 2.0 %make_messages.1 = (bf16[3,224,128]{2,1,0:T(8,128)(2,1)}, bf16[3,224,128]{2,1,0:T(8,128)(2,1)}) custom-call(f32[32,224,128]{2,1,0:T(8,128)} %get-tuple-element.42.block_ref.bottom_ref.top_ref, f32[32,224,128]{2,1,0:T(8,128)} %get-tuple-element.42.block_ref.bottom_ref.top_ref, f32[224,128]{1,0:T(8,128)} %copy-done.2, f32[224,128]{1,0:T(8,128)} %copy-done.1), custom_call_target="tpu_custom_call" | custom-call | tf_op jit(solution)/shard_map/make_messages/pallas_call | solution.py:389
  135.8 1.9 %collective-permute-start.2 = (bf16[3,224,128]{2,1,0:T(8,128)(2,1)}, bf16[3,224,128]{2,1,0:T(8,128)(2,1)S(1)}, u32[]{:S(2)}, u32[]{:S(2)}) collective-permute-start(bf16[3,224,128]{2,1,0:T(8,128)(2,1)} %get-tuple-element.45), channel_id=1, source_target_pairs={{0,8},{8,16},{16,24},{24,32},{32,40},{40,48},{48,56},{56,64},{64,7... | collective-permute-start | bytes 516104 | tf_op jit(solution)/shard_map/ppermute | solution.py:574
  137.7 6.0 %collective-permute-start.3 = (bf16[3,224,128]{2,1,0:T(8,128)(2,1)}, bf16[3,224,128]{2,1,0:T(8,128)(2,1)S(1)}, u32[]{:S(2)}, u32[]{:S(2)}) collective-permute-start(bf16[3,224,128]{2,1,0:T(8,128)(2,1)} %get-tuple-element.46), channel_id=1, source_target_pairs={{8,0},{16,8},{24,16},{32,24},{40,32},{48,40},{56,48},{64,56},{72,6... | collective-permute-start | bytes 516104 | tf_op jit(solution)/shard_map/ppermute | solution.py:574
  143.7 5.5 %diffuse_inside.1.inner_ref = f32[32,224,128]{2,1,0:T(8,128)} custom-call(f32[32,224,128]{2,1,0:T(8,128)} %get-tuple-element.42.block_ref.bottom_ref.top_ref, f32[224,128]{1,0:T(8,128)} %broadcast_in_dim.2.rate_ref, bf16[256,256]{1,0:T(8,128)(2,1)} %constant.21.clone.both_ref), custom_call_target="tpu_custom_call" | custom-call | flops 18350080 | bytes 7340032 | tf_op jit(solution)/shard_map/diffuse_inside/pallas_call | solution.py:452
  149.3 0.0 collective-permute-done.2.above_ref
  149.3 0.0 copy-start.3
  149.3 0.0 collective-permute-done.3.below_ref
  149.3 0.7 copy-done.3
  149.9 0.0 copy-start.4
  149.9 0.7 copy-done.4
  150.6 7.0 %add_borders.1 = f32[218,32,128]{2,1,0:T(8,128)} custom-call(f32[4]{0:T(128)} %add_convert_fusion.inside_ref, f32[32,224,128]{2,1,0:T(8,128)} %diffuse_inside.1.inner_ref, f32[32,224,128]{2,1,0:T(8,128)} %get-tuple-element.42.block_ref.bottom_ref.top_ref, f32[32,224,128]{2,1,0:T(8,128)} %get-tuple-element.42.block_ref.bottom_ref.top_ref, ...), custom_call_target="tpu_custom_call" | custom-call | tf_op jit(solution)/shard_map/add_borders/pallas_call | solution.py:549
Async XLA Ops:
  78.9 31.7 %all-to-all-start.1 = ((bf16[16,1,400,128]{3,2,1,0:T(8,128)(2,1)}), bf16[16,1,400,128]{3,2,1,0:T(8,128)(2,1)S(1)}, u32[]{:S(2)}, u32[]{:S(2)}) async-start(bf16[16,1,400,128]{3,2,1,0:T(8,128)(2,1)} %get-tuple-element.39), calls=%async_computation.1 | async-start | bytes 3276800 | tf_op jit(solution)/shard_map/all_to_all | solution.py:602
  110.6 1.2 copy-start
  124.9 4.6 %collective-permute-start.1 = (f32[224,128]{1,0:T(8,128)}, f32[224,128]{1,0:T(8,128)S(1)}, u32[]{:S(2)}, u32[]{:S(2)}) collective-permute-start(f32[224,128]{1,0:T(8,128)} %get-tuple-element.44.own_ref), channel_id=1, source_target_pairs={{1,0},{2,1},{3,2},{4,3},{5,4},{6,5},{7,6},{9,8},{10,9},{11,10},{12... | collective-permute-start | bytes 344072 | tf_op jit(solution)/shard_map/ppermute | solution.py:574
  126.8 6.3 %collective-permute-start = (f32[224,128]{1,0:T(8,128)}, f32[224,128]{1,0:T(8,128)S(1)}, u32[]{:S(2)}, u32[]{:S(2)}) collective-permute-start(f32[224,128]{1,0:T(8,128)} %get-tuple-element.44.own_ref), channel_id=1, source_target_pairs={{0,1},{1,2},{2,3},{3,4},{4,5},{5,6},{6,7},{8,9},{9,10},{10,11},{11... | collective-permute-start | bytes 344072 | tf_op jit(solution)/shard_map/ppermute | solution.py:574
  129.5 3.7 %copy-start.1 = (f32[224,128]{1,0:T(8,128)}, f32[224,128]{1,0:T(8,128)S(1)}, u32[]{:S(2)}) copy-start(f32[224,128]{1,0:T(8,128)S(1)} %collective-permute-done.1.high_ref) | copy-start | bytes 344068
  133.1 0.6 copy-start.2
  135.8 13.5 %collective-permute-start.2 = (bf16[3,224,128]{2,1,0:T(8,128)(2,1)}, bf16[3,224,128]{2,1,0:T(8,128)(2,1)S(1)}, u32[]{:S(2)}, u32[]{:S(2)}) collective-permute-start(bf16[3,224,128]{2,1,0:T(8,128)(2,1)} %get-tuple-element.45), channel_id=1, source_target_pairs={{0,8},{8,16},{16,24},{24,32},{32,40},{40,48},{48,56},{56,64},{64,7... | collective-permute-start | bytes 516104 | tf_op jit(solution)/shard_map/ppermute | solution.py:574
  137.7 11.6 %collective-permute-start.3 = (bf16[3,224,128]{2,1,0:T(8,128)(2,1)}, bf16[3,224,128]{2,1,0:T(8,128)(2,1)S(1)}, u32[]{:S(2)}, u32[]{:S(2)}) collective-permute-start(bf16[3,224,128]{2,1,0:T(8,128)(2,1)} %get-tuple-element.46), channel_id=1, source_target_pairs={{8,0},{16,8},{24,16},{32,24},{40,32},{48,40},{56,48},{64,56},{72,6... | collective-permute-start | bytes 516104 | tf_op jit(solution)/shard_map/ppermute | solution.py:574
  149.3 0.7 copy-start.3
  149.9 0.7 copy-start.4
